TPU v7x, 32 devices: a whole 2x2x4 slice. The times are simulated.
32 devices in a mesh: grp: 2 (over x), row: 16 (over z, y, core).
Axes of the slice: x: 2, y: 2, z: 4, core: 2. Of those that a mesh axis runs over, the one named last changes fastest.
Arguments:
- pair: bfloat16 [32, 5, 32, 2048], P(('grp', 'row')), parts along dimension 0, may hold values from -6 to 6
- kept: int32 [32, 5], P(('grp', 'row')), parts along dimension 0, may hold values from 0 to 1, as said below
- w_in: bfloat16 [64, 320], replicated, may hold values from -0.75 to 0.75
- w_out: bfloat16 [64, 64], replicated, may hold values from -0.75 to 0.75
- cotangent: bfloat16 [32, 5, 32, 2048], P(('grp', 'row')), parts along dimension 0, may hold values from -6 to 6
Outputs:
- update: bfloat16 [32, 5, 32, 2048], P(('grp', 'row')), parts along dimension 0
- grad_pair: bfloat16 [32, 5, 32, 2048], P(('grp', 'row')), parts along dimension 0
- grad_w_in: float32 [128, 320], P('grp'), parts along dimension 0
- grad_w_out: float32 [128, 64], P('grp'), parts along dimension 0
There are 2 independent parts, one for each index of `grp`. A program takes and returns all parts, laid end to end along the dimension named above; an argument that names none is the same for every part. Nothing has to cross between parts.
Inputs may be any that keep to these rules, and one draw needn't show every extreme that they name: kept[I, 2] is 1 for every block; kept[I, w] is 0 where block I + w - 2 lies outside 0 to 15; the pattern is symmetric: kept[I, w] equals kept[I + w - 2, 4 - w].
All inputs are finite; a program needn't handle non-finite values.
Results may differ from a plain program's by a relative error of at most 0.0086.
Values may be sent and summed in bfloat16 or wider, within the bound.
A program may use at most 128 MiB of HBM per device.

v0:
```python
import jax
import jax.numpy as jnp
from jax import lax
from jax.sharding import PartitionSpec as P

EPS = 1e-05


def passed_along(x, axis, by):
    devices = lax.axis_size(axis)
    pairs = [(i, i + by) for i in range(devices) if 0 <= i + by < devices]
    return lax.ppermute(x, axis, pairs)


def normalize(values):
    average = jnp.mean(values, axis=-1, keepdims=True)
    centered = values - average
    variance = jnp.mean(centered * centered, axis=-1, keepdims=True)
    return centered * lax.rsqrt(variance + EPS)


def normalize_back(values, incoming):
    average = jnp.mean(values, axis=-1, keepdims=True)
    centered = values - average
    variance = jnp.mean(centered * centered, axis=-1, keepdims=True)
    scale = lax.rsqrt(variance + EPS)
    normed = centered * scale
    return scale * (
        incoming
        - jnp.mean(incoming, axis=-1, keepdims=True)
        - normed * jnp.mean(incoming * normed, axis=-1, keepdims=True)
    )


def slot_range(offset, band_slots):
    return (max(0, offset), min(band_slots, band_slots + offset))


def project_tiles(pair_tiles, row_mask, w_in):
    channels = w_in.shape[0]
    normed = normalize(pair_tiles.astype(jnp.float32)).astype(jnp.bfloat16)
    projected = jnp.dot(normed.reshape(-1, channels), w_in, preferred_element_type=jnp.float32)
    projected = projected.reshape(pair_tiles.shape[:3] + (5 * channels,))
    gate_a, value_a, gate_b, value_b, gate_g = jnp.split(projected, 5, axis=-1)
    slot_mask = row_mask[:, None, None, None]
    left_tiles = (jax.nn.sigmoid(gate_a) * value_a * slot_mask).astype(jnp.bfloat16)
    right_tiles = (jax.nn.sigmoid(gate_b) * value_b * slot_mask).astype(jnp.bfloat16)
    return (normed, projected, left_tiles, right_tiles, jax.nn.sigmoid(gate_g))


def outgoing_product(left_part, right_part):
    return jnp.einsum("wcik,wcjk->cij", left_part, right_part, preferred_element_type=jnp.float32)


def back_product(d_tile, left_part, right_part):
    left_grad = jnp.einsum("cij,wcjk->wcik", d_tile, right_part, preferred_element_type=jnp.float32)
    right_term = jnp.einsum("cij,wcik->wcjk", d_tile, left_part, preferred_element_type=jnp.float32)
    return (left_grad, right_term.astype(jnp.bfloat16))


def local(pair, kept, w_in, w_out, cotangent):
    band_slots = pair.shape[1]
    tile_edge = pair.shape[2]
    channels = w_in.shape[0]
    half_band = band_slots // 2
    pair_tiles = pair[0].reshape(band_slots, tile_edge, tile_edge, channels)
    row_mask = kept[0].astype(jnp.float32)
    slot_mask = row_mask[:, None, None, None]
    normed, projected, left_tiles, right_tiles, gate_values = project_tiles(
        pair_tiles, row_mask, w_in
    )
    left_first = jnp.transpose(left_tiles, (0, 3, 1, 2))
    right_first = jnp.transpose(right_tiles, (0, 3, 1, 2))
    first_shape = left_first.shape
    arrived = {}
    for offset in range(-half_band, half_band + 1):
        first_slot, end_slot = slot_range(offset, band_slots)
        if offset == 0:
            arrived[offset] = right_first
        else:
            whole_band = passed_along(right_first, "row", -offset)
            arrived[offset] = whole_band[first_slot - offset : end_slot - offset]
    tri_list = []
    for out_slot in range(band_slots):
        offset = out_slot - half_band
        first_slot, end_slot = slot_range(offset, band_slots)
        left_part = left_first[first_slot:end_slot]
        tri_tile = outgoing_product(left_part, arrived[offset])
        tri_list.append(tri_tile)
    triangle = jnp.transpose(jnp.stack(tri_list), (0, 2, 3, 1))
    tri_normed = normalize(triangle).astype(jnp.bfloat16)
    mixed_out = jnp.dot(
        tri_normed.reshape(-1, channels), w_out, preferred_element_type=jnp.float32
    ).reshape(triangle.shape)
    update = (slot_mask * gate_values * mixed_out).astype(jnp.bfloat16)
    d_update = cotangent[0].reshape(pair_tiles.shape).astype(jnp.float32) * slot_mask
    d_mixed = (d_update * gate_values).astype(jnp.bfloat16)
    d_gate = d_update * mixed_out * gate_values * (1.0 - gate_values)
    grad_out_local = jnp.dot(
        tri_normed.reshape(-1, channels).T,
        d_mixed.reshape(-1, channels),
        preferred_element_type=jnp.float32,
    )
    d_tri_normed = jnp.dot(
        d_mixed.reshape(-1, channels), w_out.T, preferred_element_type=jnp.float32
    ).reshape(triangle.shape)
    d_triangle = normalize_back(triangle, d_tri_normed).astype(jnp.bfloat16)
    d_tri_first = jnp.transpose(d_triangle, (0, 3, 1, 2))
    d_left = jnp.zeros(first_shape, jnp.float32)
    d_right = jnp.zeros(first_shape, jnp.float32)
    for out_slot in range(band_slots):
        offset = out_slot - half_band
        first_slot, end_slot = slot_range(offset, band_slots)
        left_part = left_first[first_slot:end_slot]
        left_grad, right_term = back_product(d_tri_first[out_slot], left_part, arrived[offset])
        d_left = d_left.at[first_slot:end_slot].add(left_grad)
        if offset == 0:
            kept_term = lax.optimization_barrier(right_term).astype(jnp.float32)
            d_right = d_right.at[first_slot:end_slot].add(kept_term)
        else:
            padded = (
                jnp.zeros(first_shape, jnp.bfloat16)
                .at[first_slot - offset : end_slot - offset]
                .set(right_term)
            )
            d_right = d_right + passed_along(padded, "row", offset).astype(jnp.float32)
    d_left = jnp.transpose(d_left, (0, 2, 3, 1)) * slot_mask
    d_right = jnp.transpose(d_right, (0, 2, 3, 1)) * slot_mask
    gate_a, value_a, gate_b, value_b, gate_g = jnp.split(projected, 5, axis=-1)
    sig_a = jax.nn.sigmoid(gate_a)
    sig_b = jax.nn.sigmoid(gate_b)
    d_projected = jnp.concatenate(
        [
            d_left * value_a * sig_a * (1.0 - sig_a),
            d_left * sig_a,
            d_right * value_b * sig_b * (1.0 - sig_b),
            d_right * sig_b,
            d_gate,
        ],
        axis=-1,
    ).astype(jnp.bfloat16)
    flat_proj = d_projected.reshape(-1, 5 * channels)
    grad_in_local = jnp.dot(
        normed.reshape(-1, channels).T, flat_proj, preferred_element_type=jnp.float32
    )
    d_normed = jnp.dot(flat_proj, w_in.T, preferred_element_type=jnp.float32).reshape(
        pair_tiles.shape
    )
    grad_tiles = normalize_back(pair_tiles.astype(jnp.float32), d_normed).astype(jnp.bfloat16)
    grad_w_in, grad_w_out = lax.psum((grad_in_local, grad_out_local), "row")
    return (update.reshape(pair.shape), grad_tiles.reshape(pair.shape), grad_w_in, grad_w_out)


def solution(mesh):
    return jax.shard_map(
        local,
        mesh=mesh,
        in_specs=(
            P(("grp", "row"), None, None, None),
            P(("grp", "row"), None),
            P(),
            P(),
            P(("grp", "row"), None, None, None),
        ),
        out_specs=(
            P(("grp", "row"), None, None, None),
            P(("grp", "row"), None, None, None),
            P("grp", None),
            P("grp", None),
        ),
        check_vma=False,
    )
```

profile of v0, /device:TPU:0, one launch (start us, length us, event | category | flops | bytes accessed | tf_op | source)
XLA Modules:
  0.0 486.9 jit_solution(6127065303199581684)
XLA Ops:
  12.4 3.2 fusion.42
  21.9 4.1 collective-permute-start.1
  26.0 5.7 %collective-permute-start = (bf16[5,64,32,32]{1,3,2,0:T(8,128)(2,1)}, bf16[5,64,32,32]{1,3,2,0:T(8,128)(2,1)}, u32[]{:S(2)}, u32[]{:S(2)}) collective-permute-start(bf16[5,64,32,32]{1,3,2,0:T(8,128)(2,1)} %get-tuple-element.153), channel_id=1, source_target_pairs={{0,2},{1,3},{2,4},{3,5},{4,6},{5,7},{6,8},{7,9},{8,10},{9,11},{10,... | collective-permute-start | bytes 1966088 | tf_op jit(solution)/shard_map/ppermute | solution.py:12
  31.7 7.0 %copy.26 = bf16[5,64,32,32]{2,3,0,1:T(8,128)(2,1)} copy(bf16[5,64,32,32]{1,3,2,0:T(8,128)(2,1)} %get-tuple-element.153) | data formatting | bytes 1310720 | tf_op jit(solution)/shard_map/transpose | solution.py:73
  41.4 5.6 %copy.36 = bf16[5,64,32,32]{2,3,0,1:T(8,128)(2,1)} copy(bf16[5,64,32,32]{1,3,2,0:T(8,128)(2,1)S(1)} %get-tuple-element.154) | data formatting | bytes 1310720 | tf_op jit(solution)/shard_map/transpose | solution.py:72
  53.9 4.2 copy.38
  58.1 3.2 copy.34
  66.3 4.2 copy.28
  71.8 4.6 copy.24
  76.4 19.3 %collective-permute-done = bf16[5,64,32,32]{1,3,2,0:T(8,128)(2,1)} collective-permute-done((bf16[5,64,32,32]{1,3,2,0:T(8,128)(2,1)}, bf16[5,64,32,32]{1,3,2,0:T(8,128)(2,1)}, u32[]{:S(2)}, u32[]{:S(2)}) %collective-permute-start) | collective-permute-done | bytes 655392 | tf_op jit(solution)/shard_map/ppermute | solution.py:12
  113.9 5.2 %copy.19 = bf16[5,32,32,64]{3,2,1,0:T(8,128)(2,1)} copy(bf16[5,32,32,64]{2,1,3,0:T(8,128)(2,1)} %fusion.3) | data formatting | bytes 1310720 | tf_op jit(solution)/shard_map/convert_element_type | solution.py:91
  119.1 6.1 %multiply_convert_fusion.1 = (bf16[5,32,32,64]{3,2,1,0:T(8,128)(2,1)}, bf16[5,32,32,64]{3,2,1,0:T(8,128)(2,1)S(1)}, bf16[5,32,32,64]{3,2,1,0:T(8,128)(2,1)}) fusion(f32[5,32,32,64]{3,2,1,0:T(8,128)} %reshape.461, f32[5]{0:T(128)S(1)} %convert_bitcast_fusion.5, f32[5,32,32,320]{3,2,1,0:T(8,128)} %copy-done.4, bf16[5,32,32,64]{3,2,1,0:T(8,128)(2,1)} %copy.19, ...), kind=kOutput, calls=%fused_computation.36 | convolution fusion | flops 46530560 | bytes 5251092 | tf_op jit(solution)/shard_map/dot_general | solution.py:92
  128.6 7.0 %copy.20 = f32[5,32,32,64]{2,1,3,0:T(8,128)} copy(f32[5,32,32,64]{3,2,1,0:T(8,128)} %get-tuple-element.160) | data formatting | bytes 2621440 | tf_op jit(solution)/shard_map/dot_general | solution.py:104
  135.6 5.7 %multiply_reduce_fusion = f32[5,32,32]{2,1,0:T(8,128)S(1)} fusion(f32[5,32,32,64]{2,1,3,0:T(8,128)} %copy.20, f32[5,64,32,32]{3,2,1,0:T(8,128)} %copy-done.1, f32[5,32,32]{2,1,0:T(8,128)S(1)} %add_rsqrt_fusion, f32[5,32,32]{2,1,0:T(8,128)S(1)} %broadcast_multiply_fusion.4), kind=kLoop, calls=%fused_computation.5 | loop fusion | flops 1305600 | bytes 2682880 | tf_op jit(solution)/shard_map/reduce_sum | solution.py:31
  163.0 3.1 fusion.36
  166.1 83.3 %psum.15 = f32[64,64]{1,0:T(8,128)} all-reduce(f32[64,64]{1,0:T(8,128)S(1)} %convolution_bitcast_fusion.6), channel_id=1, replica_groups=mesh['grp'=2,'row'=16] {'row'}, use_global_device_ids=true, to_apply=%region_9.0 | all-reduce | flops 4096 | bytes 32768 | tf_op jit(solution)/shard_map/psum | solution.py:150
  252.4 3.6 copy.41
  255.9 5.1 %copy.39 = bf16[64,4,32,32]{0,2,3,1:T(8,128)(2,1)} copy(bf16[64,4,32,32]{3,2,1,0:T(8,128)(2,1)} %fusion.37) | data formatting | bytes 1048576 | tf_op jit(solution)/shard_map/cij,wcik->wcjk/dot_general | solution.py:57
  261.1 6.6 %copy.37 = bf16[64,5,32,32]{0,2,3,1:T(8,128)(2,1)} copy(bf16[64,5,32,32]{3,2,1,0:T(8,128)(2,1)} %fusion.35) | data formatting | bytes 1310720 | tf_op jit(solution)/shard_map/cij,wcik->wcjk/dot_general | solution.py:57
  267.7 5.1 %copy.35 = bf16[64,4,32,32]{0,2,3,1:T(8,128)(2,1)} copy(bf16[64,4,32,32]{3,2,1,0:T(8,128)(2,1)} %fusion.33) | data formatting | bytes 1048576 | tf_op jit(solution)/shard_map/cij,wcik->wcjk/dot_general | solution.py:57
  272.9 3.5 copy.33
  293.2 3.8 copy.23
  298.8 5.3 %copy.29 = f32[64,4,32,32]{0,2,3,1:T(8,128)} copy(f32[64,4,32,32]{3,2,1,0:T(8,128)} %fusion.38) | data formatting | bytes 2097152 | tf_op jit(solution)/shard_map/cij,wcjk->wcik/dot_general | solution.py:56
  304.0 5.3 %copy.25 = f32[64,4,32,32]{0,2,3,1:T(8,128)} copy(f32[64,4,32,32]{3,2,1,0:T(8,128)} %fusion.34) | data formatting | bytes 2097152 | tf_op jit(solution)/shard_map/cij,wcjk->wcik/dot_general | solution.py:56
  309.3 6.7 %copy.27 = f32[64,5,32,32]{0,2,3,1:T(8,128)} copy(f32[64,5,32,32]{3,2,1,0:T(8,128)} %fusion.36) | data formatting | bytes 2621440 | tf_op jit(solution)/shard_map/cij,wcjk->wcik/dot_general | solution.py:56
  321.9 28.5 %collective-permute-done.7 = bf16[5,64,32,32]{1,3,2,0:T(8,128)(2,1)} collective-permute-done((bf16[5,64,32,32]{1,3,2,0:T(8,128)(2,1)}, bf16[5,64,32,32]{1,3,2,0:T(8,128)(2,1)}, u32[]{:S(2)}, u32[]{:S(2)}) %collective-permute-start.7) | collective-permute-done | bytes 655392 | tf_op jit(solution)/shard_map/ppermute | solution.py:12
  350.4 6.5 %fusion.16 = (bf16[5,32,32,64]{3,2,1,0:T(8,128)(2,1)}, bf16[5,32,32,64]{3,2,1,0:T(8,128)(2,1)}, bf16[5,32,32,64]{3,2,1,0:T(8,128)(2,1)}, bf16[5,32,32,64]{3,2,1,0:T(8,128)(2,1)}) fusion(f32[5]{0:T(128)S(1)} %copy-done.35, bf16[5,64,32,32]{1,3,2,0:T(8,128)(2,1)} %collective-permute-done.7, bf16[5,64,32,32]{1,3,2,0:T(8,128)(2,1)} %collective-permute-done.6, ...), kind=kLoop, calls=%fused_computation.26 | loop fusion | flops 10158080 | bytes 12451860 | tf_op jit(solution)/shard_map/convert.5
  356.9 8.9 %concatenate.26 = bf16[5,32,32,320]{3,2,1,0:T(8,128)(2,1)} concatenate(bf16[5,32,32,64]{3,2,1,0:T(8,128)(2,1)} %get-tuple-element.151, bf16[5,32,32,64]{3,2,1,0:T(8,128)(2,1)} %get-tuple-element.152, bf16[5,32,32,64]{3,2,1,0:T(8,128)(2,1)} %get-tuple-element.145, bf16[5,32,32,64]{3,2,1,0:T(8,128)(2,1)} %get-tuple-element.144, bf16[5,32,32,64]{3,2,1,0:T(8,128)(2,1)} %get-tuple-element.146), dimensions={3} | concatenate | bytes 6553600 | tf_op jit(solution)/shard_map/concatenate | solution.py:132
  365.9 5.2 %convolution_bitcast_fusion.5 = f32[64,320]{1,0:T(8,128)} fusion(bf16[5,32,32,320]{3,2,1,0:T(8,128)(2,1)} %concatenate.26, f32[5,32,32,64]{3,2,1,0:T(8,128)S(1)} %copy-done.3, f32[5,32,32]{2,1,0:T(8,128)S(1)} %add_rsqrt_fusion.1, f32[5,32,32]{2,1,0:T(8,128)S(1)} %broadcast_multiply_fusion.5), kind=kOutput, calls=%fused_computation.63 | convolution fusion | flops 210698240 | bytes 4710400 | tf_op jit(solution)/shard_map/dot_general | solution.py:143
  371.1 6.1 %fusion.51 = (f32[5,32,32]{2,1,0:T(8,128)S(1)}, f32[5,32,32]{2,1,0:T(8,128)S(1)}, f32[5,32,32,64]{3,2,1,0:T(8,128)}) fusion(f32[5,32,32]{2,1,0:T(8,128)S(1)} %add_rsqrt_fusion.1, f32[5,32,32,64]{3,2,1,0:T(8,128)S(1)} %copy-done.3, f32[5,32,32]{2,1,0:T(8,128)S(1)} %broadcast_multiply_fusion.5, bf16[5,32,32,320]{3,2,1,0:T(8,128)(2,1)} %concatenate.26, ...), kind=kOutput, calls=%fused_computation.102 | convolution fusion | flops 211343360 | bytes 6021120 | tf_op jit(solution)/shard_map/dot_general | solution.py:146
  377.2 7.1 %multiply_convert_fusion = bf16[5,32,32,64]{3,2,1,0:T(8,128)(2,1)} fusion(f32[5,32,32,64]{3,2,1,0:T(8,128)} %get-tuple-element.161, f32[5,32,32,64]{3,2,1,0:T(8,128)S(1)} %copy-done.3, f32[5,32,32]{2,1,0:T(8,128)S(1)} %get-tuple-element.162, f32[5,32,32]{2,1,0:T(8,128)S(1)} %get-tuple-element.163, f32[5,32,32]{2,1,0:T(8,128)S(1)} %add_rsqrt_fusion.1, ...), kind=kLoop, calls=%fused_computation.34 | loop fusion | flops 2293760 | bytes 3358720 | tf_op jit(solution)/shard_map/convert_element_type | solution.py:149
  387.3 90.7 %all-reduce.7.cloned.1.call-done = f32[64,320]{1,0:T(8,128)} async-done(((f32[64,320]{1,0:T(8,128)}), f32[64,320]{1,0:T(8,128)}) %all-reduce.7.cloned.1.call-update) | async-done | bytes 81936 | tf_op jit(solution)/shard_map/psum | solution.py:150
  (152 shorter events, 102.6 us)
Async XLA Ops:
  7.2 5.3 %copy-start = (bf16[64,320]{1,0:T(8,128)(2,1)S(1)}, bf16[64,320]{1,0:T(8,128)(2,1)}, u32[]{:S(2)}) copy-start(bf16[64,320]{1,0:T(8,128)(2,1)} %param.31) | copy-start | bytes 122884
  7.2 470.8 %all-reduce.7.cloned.1.call-start = ((), (), s32[]{:S(2)}) async-start(), calls=%async_computation | async-start | bytes 196608 | tf_op jit(solution)/shard_map/psum | solution.py:150
  7.9 111.2 %copy-start.34 = (f32[5]{0:T(128)}, f32[5]{0:T(128)S(1)}, u32[]{:S(2)}) copy-start(f32[5]{0:T(128)S(1)} %convert_bitcast_fusion.5) | copy-start | bytes 64
  15.6 3.5 copy-start.4
  19.2 19.6 %copy-start.31 = (bf16[1,5,32,2048]{3,2,1,0:T(8,128)(2,1)S(1)}, bf16[1,5,32,2048]{3,2,1,0:T(8,128)(2,1)}, u32[]{:S(2)}) copy-start(bf16[1,5,32,2048]{3,2,1,0:T(8,128)(2,1)} %param.33) | copy-start | bytes 1966084
  19.2 42.1 %collective-permute-start.3 = (bf16[5,64,32,32]{1,3,2,0:T(8,128)(2,1)}, bf16[5,64,32,32]{1,3,2,0:T(8,128)(2,1)}, u32[]{:S(2)}, u32[]{:S(2)}) collective-permute-start(bf16[5,64,32,32]{1,3,2,0:T(8,128)(2,1)} %get-tuple-element.153), channel_id=1, source_target_pairs={{2,0},{3,1},{4,2},{5,3},{6,4},{7,5},{8,6},{9,7},{10,8},{11,9},{12,... | collective-permute-start | bytes 1966088 | tf_op jit(solution)/shard_map/ppermute | solution.py:12
  20.6 44.4 %collective-permute-start.2 = (bf16[5,64,32,32]{1,3,2,0:T(8,128)(2,1)}, bf16[5,64,32,32]{1,3,2,0:T(8,128)(2,1)}, u32[]{:S(2)}, u32[]{:S(2)}) collective-permute-start(bf16[5,64,32,32]{1,3,2,0:T(8,128)(2,1)} %get-tuple-element.153), channel_id=1, source_target_pairs={{1,0},{2,1},{3,2},{4,3},{5,4},{6,5},{7,6},{8,7},{9,8},{10,9},{11,1... | collective-permute-start | bytes 1966088 | tf_op jit(solution)/shard_map/ppermute | solution.py:12
  21.9 48.6 %collective-permute-start.1 = (bf16[5,64,32,32]{1,3,2,0:T(8,128)(2,1)}, bf16[5,64,32,32]{1,3,2,0:T(8,128)(2,1)}, u32[]{:S(2)}, u32[]{:S(2)}) collective-permute-start(bf16[5,64,32,32]{1,3,2,0:T(8,128)(2,1)} %get-tuple-element.153), channel_id=1, source_target_pairs={{0,1},{1,2},{2,3},{3,4},{4,5},{5,6},{6,7},{7,8},{8,9},{9,10},{10,1... | collective-permute-start | bytes 1966088 | tf_op jit(solution)/shard_map/ppermute | solution.py:12
  26.0 69.6 %collective-permute-start = (bf16[5,64,32,32]{1,3,2,0:T(8,128)(2,1)}, bf16[5,64,32,32]{1,3,2,0:T(8,128)(2,1)}, u32[]{:S(2)}, u32[]{:S(2)}) collective-permute-start(bf16[5,64,32,32]{1,3,2,0:T(8,128)(2,1)} %get-tuple-element.153), channel_id=1, source_target_pairs={{0,2},{1,3},{2,4},{3,5},{4,6},{5,7},{6,8},{7,9},{8,10},{9,11},{10,... | collective-permute-start | bytes 1966088 | tf_op jit(solution)/shard_map/ppermute | solution.py:12
  53.9 4.2 copy-start.27
  99.4 2.6 copy-start.14
  102.0 2.5 copy-start.8
  113.9 5.2 %copy-start.33 = (bf16[64,64]{1,0:T(8,128)(2,1)S(1)}, bf16[64,64]{1,0:T(8,128)(2,1)}, u32[]{:S(2)}) copy-start(bf16[64,64]{1,0:T(8,128)(2,1)} %param.32) | copy-start | bytes 24580
  119.1 6.1 %copy-start.30 = (bf16[5,32,32,64]{3,2,1,0:T(8,128)(2,1)S(1)}, bf16[5,32,32,64]{3,2,1,0:T(8,128)(2,1)}, u32[]{:S(2)}) copy-start(bf16[5,32,32,64]{3,2,1,0:T(8,128)(2,1)} %copy.19) | copy-start | bytes 1966084
  128.6 12.7 %slice-start = ((s8[5242880]{0:T(1024)(128)(4,1)}), s8[1048576]{0:T(1024)(128)(4,1)S(1)}, s32[]{:S(2)}) async-start(s8[5242880]{0:T(1024)(128)(4,1)} %bitcast.199), calls=%async_computation.1 | async-start | bytes 2097152
  135.6 5.7 %slice-start.1 = ((s8[5242880]{0:T(1024)(128)(4,1)}), s8[4194304]{0:T(1024)(128)(4,1)S(1)}, s32[]{:S(2)}) async-start(s8[5242880]{0:T(1024)(128)(4,1)} %bitcast.199), calls=%async_computation.2 | async-start | bytes 8388608
  135.6 6.8 %copy-start.5 = (f32[5,32,32,64]{2,1,3,0:T(8,128)S(1)}, f32[5,32,32,64]{2,1,3,0:T(8,128)}, u32[]{:S(2)}) copy-start(f32[5,32,32,64]{2,1,3,0:T(8,128)} %copy.20) | copy-start | bytes 3932164
  135.6 6.8 %copy-start.32 = (f32[5,32,32]{2,1,0:T(8,128)S(1)}, f32[5,32,32]{2,1,0:T(8,128)}, u32[]{:S(2)}) copy-start(f32[5,32,32]{2,1,0:T(8,128)} %broadcast_multiply_fusion.3) | copy-start | bytes 61444
  157.6 2.7 copy-start.15
  160.3 2.7 copy-start.7
  276.4 2.7 copy-start.26
  276.4 4.0 copy-start.29
  279.0 2.6 copy-start.28
  283.0 67.4 %collective-permute-start.7 = (bf16[5,64,32,32]{1,3,2,0:T(8,128)(2,1)}, bf16[5,64,32,32]{1,3,2,0:T(8,128)(2,1)}, u32[]{:S(2)}, u32[]{:S(2)}) collective-permute-start(bf16[5,64,32,32]{1,3,2,0:T(8,128)(2,1)} %scatter.19), channel_id=1, source_target_pairs={{0,2},{1,3},{2,4},{3,5},{4,6},{5,7},{6,8},{7,9},{8,10},{9,11},{10,... | collective-permute-start | bytes 1966088 | tf_op jit(solution)/shard_map/ppermute | solution.py:12
  285.3 65.1 %collective-permute-start.4 = (bf16[5,64,32,32]{1,3,2,0:T(8,128)(2,1)}, bf16[5,64,32,32]{1,3,2,0:T(8,128)(2,1)}, u32[]{:S(2)}, u32[]{:S(2)}) collective-permute-start(bf16[5,64,32,32]{1,3,2,0:T(8,128)(2,1)} %scatter.14), channel_id=1, source_target_pairs={{2,0},{3,1},{4,2},{5,3},{6,4},{7,5},{8,6},{9,7},{10,8},{11,9},{12,... | collective-permute-start | bytes 1966088 | tf_op jit(solution)/shard_map/ppermute | solution.py:12
  286.6 63.8 %collective-permute-start.6 = (bf16[5,64,32,32]{1,3,2,0:T(8,128)(2,1)}, bf16[5,64,32,32]{1,3,2,0:T(8,128)(2,1)}, u32[]{:S(2)}, u32[]{:S(2)}) collective-permute-start(bf16[5,64,32,32]{1,3,2,0:T(8,128)(2,1)} %scatter.16), channel_id=1, source_target_pairs={{0,1},{1,2},{2,3},{3,4},{4,5},{5,6},{6,7},{7,8},{8,9},{9,10},{10,1... | collective-permute-start | bytes 1966088 | tf_op jit(solution)/shard_map/ppermute | solution.py:12
  289.0 61.4 %collective-permute-start.5 = (bf16[5,64,32,32]{1,3,2,0:T(8,128)(2,1)}, bf16[5,64,32,32]{1,3,2,0:T(8,128)(2,1)}, u32[]{:S(2)}, u32[]{:S(2)}) collective-permute-start(bf16[5,64,32,32]{1,3,2,0:T(8,128)(2,1)} %scatter.15), channel_id=1, source_target_pairs={{1,0},{2,1},{3,2},{4,3},{5,4},{6,5},{7,6},{8,7},{9,8},{10,9},{11,1... | collective-permute-start | bytes 1966088 | tf_op jit(solution)/shard_map/ppermute | solution.py:12
  318.3 32.1 %slice-start.2 = ((s8[7864320]{0:T(1024)(128)(4,1)}), s8[4194304]{0:T(1024)(128)(4,1)S(1)}, s32[]{:S(2)}) async-start(s8[7864320]{0:T(1024)(128)(4,1)} %bitcast.201), calls=%async_computation.3 | async-start | bytes 8388608
  319.9 30.5 %slice-start.3 = ((s8[7864320]{0:T(1024)(128)(4,1)}), s8[3670016]{0:T(1024)(128)(4,1)S(1)}, s32[]{:S(2)}) async-start(s8[7864320]{0:T(1024)(128)(4,1)} %bitcast.201), calls=%async_computation.4 | async-start | bytes 7340032
  320.7 29.7 %copy-start.25 = (bf16[64,5,32,32]{0,2,3,1:T(8,128)(2,1)S(1)}, bf16[64,5,32,32]{0,2,3,1:T(8,128)(2,1)}, u32[]{:S(2)}) copy-start(bf16[64,5,32,32]{0,2,3,1:T(8,128)(2,1)} %copy.37) | copy-start | bytes 1966084
  320.8 29.7 %copy-start.35 = (f32[5]{0:T(128)S(1)}, f32[5]{0:T(128)}, u32[]{:S(2)}) copy-start(f32[5]{0:T(128)} %copy-done.34) | copy-start | bytes 64
  356.9 8.9 %copy-start.3 = (f32[5,32,32,64]{3,2,1,0:T(8,128)S(1)}, f32[5,32,32,64]{3,2,1,0:T(8,128)}, u32[]{:S(2)}) copy-start(f32[5,32,32,64]{3,2,1,0:T(8,128)} %copy-done.2) | copy-start | bytes 3932164
  (17 other events, 32.1 us)
Sparse Core Ops, SparseCore 0:
  377.3 100.6 all-reduce.6
where the time goes:
time: 492 us; the launch traced here: 487 us
  local copies, waits for them, and re-layouts  145 us (29%)
  waiting for transfers between devices  138 us (28%)
  blocking collectives  83.3 us (17%)
  matrix products  49.9 us (10%)
  other arithmetic  35.3 us (7%)
  starting transfers between devices  19.9 us (4%)
  between operations  15 us (3%)
    psum x1, waiting for transfers between devices, local(): grad_w_in, grad_w_out = lax.psum((grad_in_local, grad_out_local), 'row')  90.7 us
    psum x1, blocking collectives, local(): grad_w_in, grad_w_out = lax.psum((grad_in_local, grad_out_local), 'row')  83.3 us
    ppermute x8, waiting for transfers between devices, passed_along(): return lax.ppermute(x, axis, pairs)  47.7 us
    dot_general x5, local copies, waits for them, and re-layouts, back_product(): jnp.einsum('cij,wcik->wcjk', d_tile, left_part, preferred_element_type=jn...  24 us
    dot_general x5, local copies, waits for them, and re-layouts, back_product(): jnp.einsum('cij,wcjk->wcik', d_tile, right_part, preferred_element_type=j...  23.9 us
    ppermute x8, starting transfers between devices, passed_along(): return lax.ppermute(x, axis, pairs)  19.9 us
    slice x8, local copies, waits for them, and re-layouts, local(): arrived[offset] = whole_band[first_slot - offset:end_slot - offset]  18.8 us
    slice x6, local copies, waits for them, and re-layouts, local(): left_part = left_first[first_slot:end_slot]  14.2 us
  transfers between devices with their start and end apart: 9, of which 3 were waited for; matrix products, arithmetic and copies ran while one was open for 17% of the time, Pallas kernels for 0%

commit v1 on v0

--- a/solution.py
+++ b/solution.py
@@ -1,6 +1,10 @@
+import functools
+
 import jax
 import jax.numpy as jnp
 from jax import lax
+from jax.experimental import pallas as pl
+from jax.experimental.pallas import tpu as pltpu
 from jax.sharding import PartitionSpec as P
 
 EPS = 1e-05
@@ -30,6 +34,56 @@
         - jnp.mean(incoming, axis=-1, keepdims=True)
         - normed * jnp.mean(incoming * normed, axis=-1, keepdims=True)
     )
+
+
+def row_sum_body(steps, term_ref, total_ref, sent, landed, send_sem, recv_sem):
+    me = lax.axis_index("row")
+    partners = []
+    for step in range(steps):
+        bit = 1 << step
+        partners.append(me + bit * (1 - 2 * (lax.rem(me // bit, 2))))
+    barrier = pltpu.get_barrier_semaphore()
+    for partner in partners:
+        pl.semaphore_signal(
+            barrier, inc=1, device_id={"row": partner}, device_id_type=pl.DeviceIdType.MESH
+        )
+    pl.semaphore_wait(barrier, steps)
+    total = term_ref[...]
+    for step, partner in enumerate(partners):
+        sent[step] = total
+        copy = pltpu.make_async_remote_copy(
+            src_ref=sent.at[step],
+            dst_ref=landed.at[step],
+            send_sem=send_sem.at[step],
+            recv_sem=recv_sem.at[step],
+            device_id={"row": partner},
+            device_id_type=pl.DeviceIdType.MESH,
+        )
+        copy.start()
+        copy.wait()
+        total = total + landed[step]
+    total_ref[...] = total
+
+
+def row_sum(term):
+    devices = lax.axis_size("row")
+    steps = devices.bit_length() - 1
+    if steps == 0 or devices != 1 << steps:
+        return lax.psum(term, "row")
+    whole = pl.BlockSpec(memory_space=pltpu.VMEM)
+    return pl.pallas_call(
+        functools.partial(row_sum_body, steps),
+        out_shape=jax.ShapeDtypeStruct(term.shape, term.dtype),
+        in_specs=[whole],
+        out_specs=whole,
+        scratch_shapes=[
+            pltpu.VMEM((steps,) + term.shape, term.dtype),
+            pltpu.VMEM((steps,) + term.shape, term.dtype),
+            pltpu.SemaphoreType.DMA((steps,)),
+            pltpu.SemaphoreType.DMA((steps,)),
+        ],
+        compiler_params=pltpu.CompilerParams(collective_id=0, has_side_effects=True),
+    )(term)
 
 
 def slot_range(offset, band_slots):
@@ -147,7 +201,8 @@
         pair_tiles.shape
     )
     grad_tiles = normalize_back(pair_tiles.astype(jnp.float32), d_normed).astype(jnp.bfloat16)
-    grad_w_in, grad_w_out = lax.psum((grad_in_local, grad_out_local), "row")
+    summed = row_sum(jnp.concatenate([grad_in_local, grad_out_local], axis=1))
+    grad_w_in, grad_w_out = (summed[:, : 5 * channels], summed[:, 5 * channels :])
     return (update.reshape(pair.shape), grad_tiles.reshape(pair.shape), grad_w_in, grad_w_out)
 
 

time: 492 us -> 359 us (0.73)
  waiting for transfers between devices: 138 us -> 20.4 us
  blocking collectives: 83.3 us -> 0 us
  Pallas kernels: 0 us -> 56.9 us
  starting transfers between devices: 19.9 us -> 37.1 us
  between operations: 15 us -> 1.54 us
  other arithmetic: 35.3 us -> 41.4 us
    psum x1 -> x0, waiting for transfers between devices: 90.7 us -> none  [local(): grad_w_in, grad_w_out = lax.psum((grad_in_local, grad_out_local), 'row')]
    psum x1 -> x0, blocking collectives: 83.3 us -> none  [local(): grad_w_in, grad_w_out = lax.psum((grad_in_local, grad_out_local), 'row')]
    pallas_call x0 -> x1, Pallas kernels: none -> 56.9 us  [row_sum(): pl.pallas_call(functools.partial(row_sum_body, steps), out_shape=jax.Shap...]
    ppermute x8, waiting for transfers between devices: 47.7 us -> 20.4 us  [passed_along(): return lax.ppermute(x, axis, pairs)]
    ppermute x8, starting transfers between devices: 19.9 us -> 37.1 us  [passed_along(): return lax.ppermute(x, axis, pairs)]
    unnamed x81 -> x85, local copies, waits for them, and re-layouts: 11.4 us -> 11 us
  transfers between devices with their start and end apart: 9 -> 8, of which waited for: 3 -> 2; matrix products, arithmetic and copies ran while one was open for 17% -> 26% of each run, Pallas kernels for 0% -> 0%
where the time goes in v1:
time: 359 us; the launch traced here: 354 us
  local copies, waits for them, and re-layouts  146 us (41%)
  Pallas kernels  56.9 us (16%)
  matrix products  51.6 us (14%)
  other arithmetic  41.4 us (12%)
  starting transfers between devices  37.1 us (10%)
  waiting for transfers between devices  20.4 us (6%)
    pallas_call x1, Pallas kernels, row_sum(): pl.pallas_call(functools.partial(row_sum_body, steps), out_shape=jax.Shap...  56.9 us
    ppermute x8, starting transfers between devices, passed_along(): return lax.ppermute(x, axis, pairs)  37.1 us
    dot_general x5, local copies, waits for them, and re-layouts, back_product(): jnp.einsum('cij,wcjk->wcik', d_tile, right_part, preferred_element_type=j...  24 us
    dot_general x5, local copies, waits for them, and re-layouts, back_product(): jnp.einsum('cij,wcik->wcjk', d_tile, left_part, preferred_element_type=jn...  23.3 us
    ppermute x8, waiting for transfers between devices, passed_along(): return lax.ppermute(x, axis, pairs)  20.4 us
    slice x8, local copies, waits for them, and re-layouts, local(): arrived[offset] = whole_band[first_slot - offset:end_slot - offset]  18.8 us
    slice x6, local copies, waits for them, and re-layouts, local(): left_part = left_first[first_slot:end_slot]  14.2 us
    dot_general x5, matrix products, back_product(): jnp.einsum('cij,wcjk->wcik', d_tile, right_part, preferred_element_type=j...  12.9 us
  transfers between devices with their start and end apart: 8, of which 2 were waited for; matrix products, arithmetic and copies ran while one was open for 26% of the time, Pallas kernels for 0%

profile of v1, /device:TPU:0, one launch (start us, length us, event | category | flops | bytes accessed | tf_op | source)
XLA Modules:
  0.0 354.4 jit_solution(13367038570758218741)
XLA Ops:
  15.4 4.1 %collective-permute-start.1 = (bf16[5,64,32,32]{1,3,2,0:T(8,128)(2,1)}, bf16[5,64,32,32]{1,3,2,0:T(8,128)(2,1)}, u32[]{:S(2)}, u32[]{:S(2)}) collective-permute-start(bf16[5,64,32,32]{1,3,2,0:T(8,128)(2,1)} %get-tuple-element.153), channel_id=1, source_target_pairs={{0,1},{1,2},{2,3},{3,4},{4,5},{5,6},{6,7},{7,8},{8,9},{9,10},{10,1... | collective-permute-start | bytes 1966088 | tf_op jit(solution)/shard_map/ppermute | solution.py:16
  19.5 5.7 %collective-permute-start = (bf16[5,64,32,32]{1,3,2,0:T(8,128)(2,1)}, bf16[5,64,32,32]{1,3,2,0:T(8,128)(2,1)}, u32[]{:S(2)}, u32[]{:S(2)}) collective-permute-start(bf16[5,64,32,32]{1,3,2,0:T(8,128)(2,1)} %get-tuple-element.153), channel_id=1, source_target_pairs={{0,2},{1,3},{2,4},{3,5},{4,6},{5,7},{6,8},{7,9},{8,10},{9,11},{10,... | collective-permute-start | bytes 1966088 | tf_op jit(solution)/shard_map/ppermute | solution.py:16
  25.2 7.0 %copy.26 = bf16[5,64,32,32]{2,3,0,1:T(8,128)(2,1)} copy(bf16[5,64,32,32]{1,3,2,0:T(8,128)(2,1)} %get-tuple-element.153) | data formatting | bytes 1310720 | tf_op jit(solution)/shard_map/transpose | solution.py:127
  34.9 5.6 %copy.36 = bf16[5,64,32,32]{2,3,0,1:T(8,128)(2,1)} copy(bf16[5,64,32,32]{1,3,2,0:T(8,128)(2,1)S(1)} %get-tuple-element.154) | data formatting | bytes 1310720 | tf_op jit(solution)/shard_map/transpose | solution.py:126
  47.3 4.2 %copy.38 = bf16[4,64,32,32]{2,3,0,1:T(8,128)(2,1)} copy(bf16[4,64,32,32]{1,3,2,0:T(8,128)(2,1)S(1)} %get-tuple-element.157) | data formatting | bytes 1048576 | tf_op jit(solution)/shard_map/slice | solution.py:141
  51.5 3.2 copy.34
  59.7 4.2 %copy.28 = bf16[4,64,32,32]{2,3,0,1:T(8,128)(2,1)} copy(bf16[4,64,32,32]{1,3,2,0:T(8,128)(2,1)S(1)} %slice.338) | data formatting | bytes 1048576 | tf_op jit(solution)/shard_map/slice | solution.py:136
  65.2 4.6 %copy.24 = bf16[4,64,32,32]{2,3,0,1:T(8,128)(2,1)} copy(bf16[4,64,32,32]{1,3,2,0:T(8,128)(2,1)S(1)} %slice.336) | data formatting | bytes 1048576 | tf_op jit(solution)/shard_map/slice | solution.py:136
  69.8 19.3 %collective-permute-done = bf16[5,64,32,32]{1,3,2,0:T(8,128)(2,1)} collective-permute-done((bf16[5,64,32,32]{1,3,2,0:T(8,128)(2,1)}, bf16[5,64,32,32]{1,3,2,0:T(8,128)(2,1)}, u32[]{:S(2)}, u32[]{:S(2)}) %collective-permute-start) | collective-permute-done | bytes 655392 | tf_op jit(solution)/shard_map/ppermute | solution.py:16
  107.4 5.1 %copy.19 = bf16[5,32,32,64]{3,2,1,0:T(8,128)(2,1)} copy(bf16[5,32,32,64]{2,1,3,0:T(8,128)(2,1)} %fusion.3) | data formatting | bytes 1310720 | tf_op jit(solution)/shard_map/convert_element_type | solution.py:145
  112.6 5.9 %multiply_convert_fusion.1 = (bf16[5,32,32,64]{3,2,1,0:T(8,128)(2,1)}, bf16[5,32,32,64]{3,2,1,0:T(8,128)(2,1)S(1)}, bf16[5,32,32,64]{3,2,1,0:T(8,128)(2,1)}) fusion(f32[5,32,32,64]{3,2,1,0:T(8,128)} %reshape.461, f32[5]{0:T(128)S(1)} %convert_bitcast_fusion.5, f32[5,32,32,320]{3,2,1,0:T(8,128)} %copy-done.4, bf16[5,32,32,64]{3,2,1,0:T(8,128)(2,1)} %copy.19, ...), kind=kOutput, calls=%fused_computation.36 | convolution fusion | flops 46530560 | bytes 5251092 | tf_op jit(solution)/shard_map/dot_general | solution.py:146
  121.5 7.0 %copy.20 = f32[5,32,32,64]{2,1,3,0:T(8,128)} copy(f32[5,32,32,64]{3,2,1,0:T(8,128)} %get-tuple-element.160) | data formatting | bytes 2621440 | tf_op jit(solution)/shard_map/dot_general | solution.py:158
  128.5 5.7 %multiply_reduce_fusion = f32[5,32,32]{2,1,0:T(8,128)S(1)} fusion(f32[5,32,32,64]{2,1,3,0:T(8,128)} %copy.20, f32[5,64,32,32]{3,2,1,0:T(8,128)} %copy-done.1, f32[5,32,32]{2,1,0:T(8,128)S(1)} %add_rsqrt_fusion, f32[5,32,32]{2,1,0:T(8,128)S(1)} %broadcast_multiply_fusion.4), kind=kLoop, calls=%fused_computation.5 | loop fusion | flops 1305600 | bytes 2682880 | tf_op jit(solution)/shard_map/reduce_sum | solution.py:35
  155.1 3.2 fusion.36
  158.3 3.6 %copy.41 = bf16[64,3,32,32]{0,2,3,1:T(8,128)(2,1)} copy(bf16[64,3,32,32]{3,2,1,0:T(8,128)(2,1)} %fusion.39) | data formatting | bytes 786432 | tf_op jit(solution)/shard_map/cij,wcik->wcjk/dot_general | solution.py:111
  161.8 5.1 %copy.39 = bf16[64,4,32,32]{0,2,3,1:T(8,128)(2,1)} copy(bf16[64,4,32,32]{3,2,1,0:T(8,128)(2,1)} %fusion.37) | data formatting | bytes 1048576 | tf_op jit(solution)/shard_map/cij,wcik->wcjk/dot_general | solution.py:111
  167.0 5.2 %copy.35 = bf16[64,4,32,32]{0,2,3,1:T(8,128)(2,1)} copy(bf16[64,4,32,32]{3,2,1,0:T(8,128)(2,1)} %fusion.33) | data formatting | bytes 1048576 | tf_op jit(solution)/shard_map/cij,wcik->wcjk/dot_general | solution.py:111
  172.1 3.5 copy.33
  182.2 11.2 %collective-permute-start.7 = (bf16[5,64,32,32]{1,3,2,0:T(8,128)(2,1)}, bf16[5,64,32,32]{1,3,2,0:T(8,128)(2,1)}, u32[]{:S(2)}, u32[]{:S(2)}) collective-permute-start(bf16[5,64,32,32]{1,3,2,0:T(8,128)(2,1)} %scatter.19), channel_id=1, source_target_pairs={{0,2},{1,3},{2,4},{3,5},{4,6},{5,7},{6,8},{7,9},{8,10},{9,11},{10,... | collective-permute-start | bytes 1966088 | tf_op jit(solution)/shard_map/ppermute | solution.py:16
  194.7 10.8 %collective-permute-start.6 = (bf16[5,64,32,32]{1,3,2,0:T(8,128)(2,1)}, bf16[5,64,32,32]{1,3,2,0:T(8,128)(2,1)}, u32[]{:S(2)}, u32[]{:S(2)}) collective-permute-start(bf16[5,64,32,32]{1,3,2,0:T(8,128)(2,1)} %scatter.16), channel_id=1, source_target_pairs={{0,1},{1,2},{2,3},{3,4},{4,5},{5,6},{6,7},{7,8},{8,9},{9,10},{10,1... | collective-permute-start | bytes 1966088 | tf_op jit(solution)/shard_map/ppermute | solution.py:16
  211.3 5.3 %copy.29 = f32[64,4,32,32]{0,2,3,1:T(8,128)} copy(f32[64,4,32,32]{3,2,1,0:T(8,128)} %fusion.38) | data formatting | bytes 2097152 | tf_op jit(solution)/shard_map/cij,wcjk->wcik/dot_general | solution.py:110
  216.6 5.3 %copy.25 = f32[64,4,32,32]{0,2,3,1:T(8,128)} copy(f32[64,4,32,32]{3,2,1,0:T(8,128)} %fusion.34) | data formatting | bytes 2097152 | tf_op jit(solution)/shard_map/cij,wcjk->wcik/dot_general | solution.py:110
  221.9 6.7 %copy.27 = f32[64,5,32,32]{0,2,3,1:T(8,128)} copy(f32[64,5,32,32]{3,2,1,0:T(8,128)} %fusion.36) | data formatting | bytes 2621440 | tf_op jit(solution)/shard_map/cij,wcjk->wcik/dot_general | solution.py:110
  234.7 3.9 %fusion.40 = f32[64,3,32,32]{3,2,1,0:T(8,128)} fusion(bf16[3,64,32,32]{2,3,0,1:T(8,128)(2,1)S(1)} %copy-done.24, bf16[5,64,32,32]{3,2,1,0:T(8,128)(2,1)} %copy-done.11), kind=kOutput, calls=%fused_computation.83 | convolution fusion | flops 12582912 | bytes 1703936 | tf_op jit(solution)/shard_map/cij,wcjk->wcik/dot_general | solution.py:110
  241.5 5.9 %copy.37 = bf16[64,5,32,32]{0,2,3,1:T(8,128)(2,1)} copy(bf16[64,5,32,32]{3,2,1,0:T(8,128)(2,1)S(1)} %copy-done.26) | data formatting | bytes 1310720 | tf_op jit(solution)/shard_map/cij,wcik->wcjk/dot_general | solution.py:111
  247.5 4.0 %copy.31 = f32[64,3,32,32]{0,2,3,1:T(8,128)} copy(f32[64,3,32,32]{3,2,1,0:T(8,128)} %fusion.40) | data formatting | bytes 1572864 | tf_op jit(solution)/shard_map/cij,wcjk->wcik/dot_general | solution.py:110
  256.9 9.4 %fusion.16 = (bf16[5,32,32,64]{3,2,1,0:T(8,128)(2,1)}, bf16[5,32,32,64]{3,2,1,0:T(8,128)(2,1)}, bf16[5,32,32,64]{3,2,1,0:T(8,128)(2,1)}, bf16[5,32,32,64]{3,2,1,0:T(8,128)(2,1)}) fusion(f32[5]{0:T(128)S(1)} %convert_bitcast_fusion.5, bf16[5,64,32,32]{1,3,2,0:T(8,128)(2,1)} %collective-permute-done.7, bf16[5,64,32,32]{1,3,2,0:T(8,128)(2,1)} %collective-permute-done.6, ...), kind=kLoop, calls=%fused_computation.26 | loop fusion | flops 10158080 | bytes 12451860 | tf_op jit(solution)/shard_map/convert.5
  266.2 8.9 %concatenate.29 = bf16[5,32,32,320]{3,2,1,0:T(8,128)(2,1)} concatenate(bf16[5,32,32,64]{3,2,1,0:T(8,128)(2,1)} %get-tuple-element.151, bf16[5,32,32,64]{3,2,1,0:T(8,128)(2,1)} %get-tuple-element.152, bf16[5,32,32,64]{3,2,1,0:T(8,128)(2,1)} %get-tuple-element.145, bf16[5,32,32,64]{3,2,1,0:T(8,128)(2,1)} %get-tuple-element.144, bf16[5,32,32,64]{3,2,1,0:T(8,128)(2,1)} %get-tuple-element.146), dimensions={3} | concatenate | bytes 6553600 | tf_op jit(solution)/shard_map/concatenate | solution.py:186
  275.2 4.8 %convolution_bitcast_fusion.5 = f32[64,320]{1,0:T(8,128)S(1)} fusion(bf16[5,32,32,320]{3,2,1,0:T(8,128)(2,1)} %concatenate.29, f32[5,32,32,64]{3,2,1,0:T(8,128)S(1)} %copy-done.3, f32[5,32,32]{2,1,0:T(8,128)S(1)} %add_rsqrt_fusion.1, f32[5,32,32]{2,1,0:T(8,128)S(1)} %broadcast_multiply_fusion.5), kind=kOutput, calls=%fused_computation.63 | convolution fusion | flops 210698240 | bytes 4710400 | tf_op jit(solution)/shard_map/dot_general | solution.py:197
  279.9 4.2 %fusion.51 = (f32[5,32,32]{2,1,0:T(8,128)S(1)}, f32[5,32,32]{2,1,0:T(8,128)S(1)}, f32[5,32,32,64]{3,2,1,0:T(8,128)}) fusion(f32[5,32,32]{2,1,0:T(8,128)S(1)} %add_rsqrt_fusion.1, f32[5,32,32,64]{3,2,1,0:T(8,128)S(1)} %copy-done.3, f32[5,32,32]{2,1,0:T(8,128)S(1)} %broadcast_multiply_fusion.5, bf16[5,32,32,320]{3,2,1,0:T(8,128)(2,1)S(1)} %copy-done.6, ...), kind=kOutput, calls=%fused_computation.103 | convolution fusion | flops 211343360 | bytes 6021120 | tf_op jit(solution)/shard_map/dot_general | solution.py:200
  284.8 56.9 %shard_map.94 = f32[64,384]{1,0:T(8,128)} custom-call(f32[64,384]{1,0:T(8,128)} %pad_maximum_fusion.term_ref), custom_call_target="tpu_custom_call" | custom-call | tf_op jit(solution)/shard_map/pallas_call | solution.py:74
  343.2 7.1 %multiply_convert_fusion = bf16[5,32,32,64]{3,2,1,0:T(8,128)(2,1)} fusion(f32[5,32,32,64]{3,2,1,0:T(8,128)} %get-tuple-element.161, f32[5,32,32,64]{3,2,1,0:T(8,128)S(1)} %copy-done.3, f32[5,32,32]{2,1,0:T(8,128)S(1)} %broadcast_multiply_fusion, f32[5,32,32]{2,1,0:T(8,128)S(1)} %broadcast_multiply_fusion.1, f32[5,32,32]{2,1,0:T(8,128)S(1)} %add_rsqrt_fusion.1, ...), kind=kLoop, calls=%fused_computation.34 | loop fusion | flops 2293760 | bytes 3358720 | tf_op jit(solution)/shard_map/convert_element_type | solution.py:203
  (154 shorter events, 106.5 us)
Async XLA Ops:
  0.6 5.2 %copy-start = (bf16[64,320]{1,0:T(8,128)(2,1)S(1)}, bf16[64,320]{1,0:T(8,128)(2,1)}, u32[]{:S(2)}) copy-start(bf16[64,320]{1,0:T(8,128)(2,1)} %param.31) | copy-start | bytes 122884
  9.0 3.6 %copy-start.4 = (f32[5,32,32,320]{3,2,1,0:T(8,128)}, f32[5,32,32,320]{3,2,1,0:T(8,128)S(1)}, u32[]{:S(2)}) copy-start(f32[5,32,32,320]{3,2,1,0:T(8,128)S(1)} %fusion.42) | copy-start | bytes 19660804
  12.7 19.5 %copy-start.36 = (bf16[1,5,32,2048]{3,2,1,0:T(8,128)(2,1)S(1)}, bf16[1,5,32,2048]{3,2,1,0:T(8,128)(2,1)}, u32[]{:S(2)}) copy-start(bf16[1,5,32,2048]{3,2,1,0:T(8,128)(2,1)} %param.33) | copy-start | bytes 1966084
  12.7 42.1 %collective-permute-start.3 = (bf16[5,64,32,32]{1,3,2,0:T(8,128)(2,1)}, bf16[5,64,32,32]{1,3,2,0:T(8,128)(2,1)}, u32[]{:S(2)}, u32[]{:S(2)}) collective-permute-start(bf16[5,64,32,32]{1,3,2,0:T(8,128)(2,1)} %get-tuple-element.153), channel_id=1, source_target_pairs={{2,0},{3,1},{4,2},{5,3},{6,4},{7,5},{8,6},{9,7},{10,8},{11,9},{12,... | collective-permute-start | bytes 1966088 | tf_op jit(solution)/shard_map/ppermute | solution.py:16
  14.1 44.4 %collective-permute-start.2 = (bf16[5,64,32,32]{1,3,2,0:T(8,128)(2,1)}, bf16[5,64,32,32]{1,3,2,0:T(8,128)(2,1)}, u32[]{:S(2)}, u32[]{:S(2)}) collective-permute-start(bf16[5,64,32,32]{1,3,2,0:T(8,128)(2,1)} %get-tuple-element.153), channel_id=1, source_target_pairs={{1,0},{2,1},{3,2},{4,3},{5,4},{6,5},{7,6},{8,7},{9,8},{10,9},{11,1... | collective-permute-start | bytes 1966088 | tf_op jit(solution)/shard_map/ppermute | solution.py:16
  15.4 48.5 %collective-permute-start.1 = (bf16[5,64,32,32]{1,3,2,0:T(8,128)(2,1)}, bf16[5,64,32,32]{1,3,2,0:T(8,128)(2,1)}, u32[]{:S(2)}, u32[]{:S(2)}) collective-permute-start(bf16[5,64,32,32]{1,3,2,0:T(8,128)(2,1)} %get-tuple-element.153), channel_id=1, source_target_pairs={{0,1},{1,2},{2,3},{3,4},{4,5},{5,6},{6,7},{7,8},{8,9},{9,10},{10,1... | collective-permute-start | bytes 1966088 | tf_op jit(solution)/shard_map/ppermute | solution.py:16
  19.5 69.6 %collective-permute-start = (bf16[5,64,32,32]{1,3,2,0:T(8,128)(2,1)}, bf16[5,64,32,32]{1,3,2,0:T(8,128)(2,1)}, u32[]{:S(2)}, u32[]{:S(2)}) collective-permute-start(bf16[5,64,32,32]{1,3,2,0:T(8,128)(2,1)} %get-tuple-element.153), channel_id=1, source_target_pairs={{0,2},{1,3},{2,4},{3,5},{4,6},{5,7},{6,8},{7,9},{8,10},{9,11},{10,... | collective-permute-start | bytes 1966088 | tf_op jit(solution)/shard_map/ppermute | solution.py:16
  47.3 4.2 %copy-start.32 = (bf16[4,64,32,32]{1,3,2,0:T(8,128)(2,1)S(1)}, bf16[4,64,32,32]{1,3,2,0:T(8,128)(2,1)}, u32[]{:S(2)}) copy-start(bf16[4,64,32,32]{1,3,2,0:T(8,128)(2,1)} %get-tuple-element.158) | copy-start | bytes 1572868
  92.8 2.6 copy-start.18
  107.4 5.2 %copy-start.39 = (bf16[64,64]{1,0:T(8,128)(2,1)S(1)}, bf16[64,64]{1,0:T(8,128)(2,1)}, u32[]{:S(2)}) copy-start(bf16[64,64]{1,0:T(8,128)(2,1)} %param.32) | copy-start | bytes 24580
  118.5 3.0 copy-start.35
  121.5 12.8 %slice-start = ((s8[5242880]{0:T(1024)(128)(4,1)}), s8[1048576]{0:T(1024)(128)(4,1)S(1)}, s32[]{:S(2)}) async-start(s8[5242880]{0:T(1024)(128)(4,1)} %bitcast.200), calls=%async_computation | async-start | bytes 2097152
  128.5 5.7 %copy-start.38 = (f32[5,32,32]{2,1,0:T(8,128)S(1)}, f32[5,32,32]{2,1,0:T(8,128)}, u32[]{:S(2)}) copy-start(f32[5,32,32]{2,1,0:T(8,128)} %get-tuple-element.159) | copy-start | bytes 61444
  128.5 5.8 %slice-start.1 = ((s8[5242880]{0:T(1024)(128)(4,1)}), s8[4194304]{0:T(1024)(128)(4,1)S(1)}, s32[]{:S(2)}) async-start(s8[5242880]{0:T(1024)(128)(4,1)} %bitcast.200), calls=%async_computation.1 | async-start | bytes 8388608
  128.5 6.8 %copy-start.5 = (f32[5,32,32,64]{2,1,3,0:T(8,128)S(1)}, f32[5,32,32,64]{2,1,3,0:T(8,128)}, u32[]{:S(2)}) copy-start(f32[5,32,32,64]{2,1,3,0:T(8,128)} %copy.20) | copy-start | bytes 3932164
  136.9 18.1 %copy-start.11 = (bf16[5,64,32,32]{3,2,1,0:T(8,128)(2,1)}, bf16[5,64,32,32]{3,2,1,0:T(8,128)(2,1)S(1)}, u32[]{:S(2)}) copy-start(bf16[5,64,32,32]{3,2,1,0:T(8,128)(2,1)S(1)} %fusion.1) | copy-start | bytes 1966084
  137.0 3.1 copy-start.15
  149.8 2.7 copy-start.19
  152.4 2.6 copy-start.8
  175.7 2.7 copy-start.31
  175.7 4.0 %copy-start.34 = (bf16[64,3,32,32]{0,2,3,1:T(8,128)(2,1)S(1)}, bf16[64,3,32,32]{0,2,3,1:T(8,128)(2,1)}, u32[]{:S(2)}) copy-start(bf16[64,3,32,32]{0,2,3,1:T(8,128)(2,1)} %copy.33) | copy-start | bytes 1179652
  182.2 74.6 %collective-permute-start.7 = (bf16[5,64,32,32]{1,3,2,0:T(8,128)(2,1)}, bf16[5,64,32,32]{1,3,2,0:T(8,128)(2,1)}, u32[]{:S(2)}, u32[]{:S(2)}) collective-permute-start(bf16[5,64,32,32]{1,3,2,0:T(8,128)(2,1)} %scatter.19), channel_id=1, source_target_pairs={{0,2},{1,3},{2,4},{3,5},{4,6},{5,7},{6,8},{7,9},{8,10},{9,11},{10,... | collective-permute-start | bytes 1966088 | tf_op jit(solution)/shard_map/ppermute | solution.py:16
  193.4 63.4 %collective-permute-start.4 = (bf16[5,64,32,32]{1,3,2,0:T(8,128)(2,1)}, bf16[5,64,32,32]{1,3,2,0:T(8,128)(2,1)}, u32[]{:S(2)}, u32[]{:S(2)}) collective-permute-start(bf16[5,64,32,32]{1,3,2,0:T(8,128)(2,1)} %scatter.14), channel_id=1, source_target_pairs={{2,0},{3,1},{4,2},{5,3},{6,4},{7,5},{8,6},{9,7},{10,8},{11,9},{12,... | collective-permute-start | bytes 1966088 | tf_op jit(solution)/shard_map/ppermute | solution.py:16
  194.7 62.1 %collective-permute-start.6 = (bf16[5,64,32,32]{1,3,2,0:T(8,128)(2,1)}, bf16[5,64,32,32]{1,3,2,0:T(8,128)(2,1)}, u32[]{:S(2)}, u32[]{:S(2)}) collective-permute-start(bf16[5,64,32,32]{1,3,2,0:T(8,128)(2,1)} %scatter.16), channel_id=1, source_target_pairs={{0,1},{1,2},{2,3},{3,4},{4,5},{5,6},{6,7},{7,8},{8,9},{9,10},{10,1... | collective-permute-start | bytes 1966088 | tf_op jit(solution)/shard_map/ppermute | solution.py:16
  205.5 51.4 %collective-permute-start.5 = (bf16[5,64,32,32]{1,3,2,0:T(8,128)(2,1)}, bf16[5,64,32,32]{1,3,2,0:T(8,128)(2,1)}, u32[]{:S(2)}, u32[]{:S(2)}) collective-permute-start(bf16[5,64,32,32]{1,3,2,0:T(8,128)(2,1)} %scatter.15), channel_id=1, source_target_pairs={{1,0},{2,1},{3,2},{4,3},{5,4},{6,5},{7,6},{8,7},{9,8},{10,9},{11,1... | collective-permute-start | bytes 1966088 | tf_op jit(solution)/shard_map/ppermute | solution.py:16
  234.7 3.9 %copy-start.12 = (f32[5,64,32,32]{1,3,2,0:T(8,128)}, f32[5,64,32,32]{1,3,2,0:T(8,128)S(1)}, u32[]{:S(2)}) copy-start(f32[5,64,32,32]{1,3,2,0:T(8,128)S(1)} %get-tuple-element.142) | copy-start | bytes 3932164
  234.7 6.8 %copy-start.26 = (bf16[64,5,32,32]{3,2,1,0:T(8,128)(2,1)S(1)}, bf16[64,5,32,32]{3,2,1,0:T(8,128)(2,1)}, u32[]{:S(2)}) copy-start(bf16[64,5,32,32]{3,2,1,0:T(8,128)(2,1)} %fusion.35) | copy-start | bytes 1966084
  247.5 6.4 %copy-start.13 = (f32[5,64,32,32]{1,3,2,0:T(8,128)S(1)}, f32[5,64,32,32]{1,3,2,0:T(8,128)}, u32[]{:S(2)}) copy-start(f32[5,64,32,32]{1,3,2,0:T(8,128)} %copy-done.12) | copy-start | bytes 3932164
  253.8 3.0 copy-start.30
  266.2 8.9 %copy-start.3 = (f32[5,32,32,64]{3,2,1,0:T(8,128)S(1)}, f32[5,32,32,64]{3,2,1,0:T(8,128)}, u32[]{:S(2)}) copy-start(f32[5,32,32,64]{3,2,1,0:T(8,128)} %copy-done.2) | copy-start | bytes 3932164
  275.2 4.8 %copy-start.6 = (bf16[5,32,32,320]{3,2,1,0:T(8,128)(2,1)S(1)}, bf16[5,32,32,320]{3,2,1,0:T(8,128)(2,1)}, u32[]{:S(2)}) copy-start(bf16[5,32,32,320]{3,2,1,0:T(8,128)(2,1)} %concatenate.29) | copy-start | bytes 9830404
  343.2 10.1 %copy-start.37 = (f32[64,384]{1,0:T(8,128)S(1)}, f32[64,384]{1,0:T(8,128)}, u32[]{:S(2)}) copy-start(f32[64,384]{1,0:T(8,128)} %shard_map.94) | copy-start | bytes 294916
  (18 other events, 36.4 us)

commit v2 on v0

v2 whole, which is shorter than its diff:
```python
import functools

import jax
import jax.numpy as jnp
from jax import lax
from jax.experimental import pallas as pl
from jax.experimental.pallas import tpu as pltpu
from jax.sharding import PartitionSpec as P

EPS = 1e-05
F32 = jnp.float32
BF16 = jnp.bfloat16
NN = (((1,), (0,)), ((), ()))
NT = (((1,), (1,)), ((), ()))
TN = (((0,), (0,)), ((), ()))


def dot(a, b, dims):
    return lax.dot_general(a, b, dims, preferred_element_type=F32)


def unit(values):
    average = jnp.mean(values, axis=0, keepdims=True)
    centered = values - average
    variance = jnp.mean(centered * centered, axis=0, keepdims=True)
    scale = lax.rsqrt(variance + EPS)
    return centered * scale, scale


def unit_back(normed, scale, incoming):
    return scale * (
        incoming
        - jnp.mean(incoming, axis=0, keepdims=True)
        - normed * jnp.mean(incoming * normed, axis=0, keepdims=True)
    )


def gated(projected, channels, group):
    gate = jax.nn.sigmoid(projected[2 * group * channels : (2 * group + 1) * channels])
    return gate * projected[(2 * group + 1) * channels : (2 * group + 2) * channels]


def taken(ref, rows, wide, *first):
    lanes = ref.shape[-1]
    chunks = [ref[(*first, k, rows, slice(None))] for k in range(ref.shape[-3])]
    return jnp.concatenate(chunks, axis=1)[:, :wide] if len(chunks) * lanes > wide else chunks[0]


def put(ref, rows, values, *first):
    lanes = ref.shape[-1]
    short = ref.shape[-3] * lanes - values.shape[1]
    if short > 0:
        values = jnp.concatenate([values, jnp.zeros((values.shape[0], short), F32)], axis=1)
    for k in range(ref.shape[-3]):
        ref[(*first, k, rows, slice(None))] = values[:, k * lanes : (k + 1) * lanes]


def body(
    devices,
    slots,
    edge,
    channels,
    own_ref, s0, s1, s2, s3, cot_ref, mask_ref, w_in_ref, w_in_t_ref, w_out_ref, w_out_t_ref,
    update_ref, grad_ref, weights_ref,
    slabs, left, right, band, gates, d_gates, tri, d_left, d_right, packed, arrived, spread,
    terms, landed, slab_send, slab_recv, pack_send, pack_recv, sum_send, sum_recv,
):
    half = slots // 2
    rows = edge * channels
    wide = slots * edge
    lanes = slabs.shape[2]
    folds = lanes // edge
    steps = devices.bit_length() - 1
    offsets = [d for d in range(-half, half + 1) if d != 0]
    slab_refs = dict(zip(offsets, (s0, s1, s2, s3)))
    me = lax.axis_index("row")

    def there(d):
        return jnp.logical_and(me + d >= 0, me + d < devices)

    partners = []
    for step in range(steps):
        bit = 1 << step
        partners.append(me + bit * (1 - 2 * lax.rem(me // bit, 2)))

    def greet(target):
        pl.semaphore_signal(
            barrier, inc=1, device_id={"row": target}, device_id_type=pl.DeviceIdType.MESH
        )

    barrier = pltpu.get_barrier_semaphore()
    for d in offsets:
        pl.when(there(d))(functools.partial(greet, me + d))
    for partner in partners:
        greet(partner)
    pl.semaphore_wait(barrier, steps + sum(there(d).astype(jnp.int32) for d in offsets))

    def slab_copy(d):
        return pltpu.make_async_remote_copy(
            src_ref=slab_refs[d],
            dst_ref=slabs.at[offsets.index(-d)],
            send_sem=slab_send.at[offsets.index(d)],
            recv_sem=slab_recv.at[offsets.index(-d)],
            device_id={"row": me + d},
            device_id_type=pl.DeviceIdType.MESH,
        )

    def slab_arrival(d):
        return pltpu.make_async_remote_copy(
            src_ref=slab_refs[d],
            dst_ref=slabs.at[offsets.index(d)],
            send_sem=slab_send.at[offsets.index(d)],
            recv_sem=slab_recv.at[offsets.index(d)],
            device_id={"row": me + d},
            device_id_type=pl.DeviceIdType.MESH,
        )

    def pack_copy(d, landing):
        return pltpu.make_async_remote_copy(
            src_ref=packed.at[offsets.index(d)],
            dst_ref=arrived.at[offsets.index(landing)],
            send_sem=pack_send.at[offsets.index(d)],
            recv_sem=pack_recv.at[offsets.index(landing)],
            device_id={"row": me + d},
            device_id_type=pl.DeviceIdType.MESH,
        )

    for d in offsets:
        pl.when(there(d))(lambda d=d: slab_copy(d).start())

    w_in = w_in_ref[...]
    w_in_t = w_in_t_ref[...]
    w_out = w_out_ref[...]
    w_out_t = w_out_t_ref[...]
    mask = mask_ref[...]

    def at(i):
        return pl.ds(pl.multiple_of(i * channels, channels), channels)

    def project_own(i, carry):
        normed, _ = unit(own_ref[at(i), :].astype(F32))
        projected = dot(w_in_t, normed.astype(BF16), NN)
        put(left, at(i), gated(projected, channels, 0).astype(BF16).astype(F32), half)
        put(right, at(i), gated(projected, channels, 1).astype(BF16).astype(F32), half)
        gates[at(i), :] = jax.nn.sigmoid(projected[4 * channels :])
        return carry

    lax.fori_loop(0, edge, project_own, 0)

    for d in offsets:
        index = offsets.index(d)
        count = slots - abs(d)
        first = max(0, d) * edge

        def absent(index=index):
            slabs[index] = jnp.zeros((rows, lanes), BF16)

        pl.when(there(d))(lambda d=d: slab_arrival(d).wait_recv())
        pl.when(jnp.logical_not(there(d)))(absent)

        def placed(values, first=first, count=count):
            values = values[:, : count * edge]
            parts = [values]
            if first > 0:
                parts = [jnp.zeros((channels, first), F32)] + parts
            tail = wide - first - count * edge
            if tail > 0:
                parts = parts + [jnp.zeros((channels, tail), F32)]
            return jnp.concatenate(parts, axis=1)

        def project_far(i, carry, d=d, index=index, placed=placed):
            normed, _ = unit(slabs[index, at(i), :].astype(F32))
            projected = dot(w_in_t[: 4 * channels], normed.astype(BF16), NN)
            for group, ref in enumerate((left, right)):
                values = placed(gated(projected, channels, group)).astype(BF16).astype(F32)
                put(ref, at(i), values, half + d)
            return carry

        lax.fori_loop(0, edge, project_far, 0)

    def triangle(c, carry):
        every = pl.ds(c, edge, stride=channels)
        block = jnp.concatenate([taken(right, every, wide, v) for v in range(slots)], axis=0).astype(BF16)
        band[c] = block
        put(tri, every, dot(taken(left, every, wide, half).astype(BF16), block, NT))
        return carry

    lax.fori_loop(0, channels, triangle, 0)

    def middle(start, carry):
        total = carry
        d_tiles = []
        for fold in range(folds):
            i = start + fold * (edge // folds)
            normed, scale = unit(taken(tri, at(i), wide))
            normed_low = normed.astype(BF16)
            mixed = dot(w_out_t, normed_low, NN)
            gate = gates[at(i), :]
            update_ref[at(i), :] = (mask * gate * mixed).astype(BF16)
            d_update = cot_ref[at(i), :].astype(F32) * mask
            d_mixed = (d_update * gate).astype(BF16)
            d_gates[at(i), :] = d_update * mixed * gate * (1.0 - gate)
            total = total + dot(normed_low, d_mixed, NT)
            d_tri = unit_back(normed, scale, dot(w_out, d_mixed, NN)).astype(BF16).astype(F32)
            put(tri, at(i), d_tri)
            d_tiles.append(d_tri)
        for d in offsets:
            v = half + d
            packed[offsets.index(d), at(start), :] = jnp.concatenate(
                [tile[:, v * edge : (v + 1) * edge] for tile in d_tiles], axis=1
            ).astype(BF16)
        return total

    grad_out = lax.fori_loop(0, edge // folds, middle, jnp.zeros((channels, channels), F32))

    for d in offsets:
        pl.when(there(d))(lambda d=d: pack_copy(d, -d).start())

    def to_left(c, carry):
        every = pl.ds(c, edge, stride=channels)
        put(d_left, every, dot(taken(tri, every, wide).astype(BF16), band[c], NN))
        return carry

    lax.fori_loop(0, channels, to_left, 0)

    for d in offsets:
        index = offsets.index(d)

        def absent(index=index):
            arrived[index] = jnp.zeros(arrived.shape[1:], BF16)

        pl.when(there(d))(lambda d=d: pack_copy(d, d).wait_recv())
        pl.when(jnp.logical_not(there(d)))(absent)
        spread[index] = arrived[index].astype(F32)

    def to_right(c, carry):
        every = pl.ds(c, edge, stride=channels)
        folded = pl.ds(c, edge // folds, stride=channels)
        pieces = []
        sources = []
        for d in range(-half, half + 1):
            sources.append(taken(left, every, wide, half + d))
            if d == 0:
                pieces.append(taken(tri, every, wide)[:, half * edge : (half + 1) * edge])
            else:
                tile = spread[offsets.index(d), folded, :]
                for fold in range(folds):
                    pieces.append(tile[:, fold * edge : (fold + 1) * edge])
        d_tile = jnp.concatenate(pieces, axis=0).astype(BF16)
        source = jnp.concatenate(sources, axis=0).astype(BF16)
        put(d_right, every, dot(d_tile, source, TN))
        return carry

    lax.fori_loop(0, channels, to_right, 0)

    def last(i, carry):
        normed, scale = unit(own_ref[at(i), :].astype(F32))
        normed_low = normed.astype(BF16)
        projected = dot(w_in_t[: 4 * channels], normed_low, NN)
        parts = []
        for group, ref in enumerate((d_left, d_right)):
            gate = jax.nn.sigmoid(projected[2 * group * channels : (2 * group + 1) * channels])
            value = projected[(2 * group + 1) * channels : (2 * group + 2) * channels]
            to_value = taken(ref, at(i), wide) * mask * gate
            parts.append(to_value * value * (1.0 - gate))
            parts.append(to_value)
        parts.append(d_gates[at(i), :])
        d_projected = jnp.concatenate(parts, axis=0).astype(BF16)
        grad_ref[at(i), :] = unit_back(normed, scale, dot(w_in, d_projected, NN)).astype(BF16)
        return carry + dot(d_projected, normed_low, NT)

    grad_in = lax.fori_loop(0, edge, last, jnp.zeros((5 * channels, channels), F32))

    total = jnp.concatenate([grad_in, grad_out], axis=0)
    for step, partner in enumerate(partners):
        terms[step] = total
        copy = pltpu.make_async_remote_copy(
            src_ref=terms.at[step],
            dst_ref=landed.at[step],
            send_sem=sum_send.at[step],
            recv_sem=sum_recv.at[step],
            device_id={"row": partner},
            device_id_type=pl.DeviceIdType.MESH,
        )
        copy.start()
        copy.wait()
        total = total + landed[step]
    weights_ref[...] = total

    for d in offsets:
        pl.when(there(d))(lambda d=d: slab_copy(d).wait_send())
        pl.when(there(d))(lambda d=d: pack_copy(d, -d).wait_send())


def local(pair, kept, w_in, w_out, cotangent):
    slots, edge = pair.shape[1], pair.shape[2]
    channels = w_in.shape[0]
    half = slots // 2
    rows, wide = edge * channels, slots * edge
    lanes = 128
    chunks = -(-wide // lanes)
    devices = lax.axis_size("row")
    steps = devices.bit_length() - 1

    def to_columns(tiles):
        return jnp.transpose(tiles, (1, 3, 0, 2)).reshape(rows, wide)

    def from_columns(columns):
        tiles = columns.reshape(edge, channels, slots, edge)
        return jnp.transpose(tiles, (2, 0, 3, 1)).reshape(pair.shape)

    tiles = pair[0].reshape(slots, edge, edge, channels)
    own = to_columns(tiles * kept[0].astype(BF16)[:, None, None, None])
    cot = to_columns(cotangent[0].reshape(tiles.shape))
    mask = jnp.repeat(kept[0].astype(F32), edge)[None, :]
    slabs = []
    for d in range(-half, half + 1):
        if d != 0:
            low = max(0, d) * edge
            count = (slots - abs(d)) * edge
            slab = own[:, low : low + count]
            slabs.append(jnp.pad(slab, ((0, 0), (0, lanes - count))))

    whole = pl.BlockSpec(memory_space=pltpu.VMEM)
    far = len(slabs)
    update, grad, weights = pl.pallas_call(
        functools.partial(body, devices, slots, edge, channels),
        out_shape=(
            jax.ShapeDtypeStruct((rows, wide), BF16),
            jax.ShapeDtypeStruct((rows, wide), BF16),
            jax.ShapeDtypeStruct((6 * channels, channels), F32),
        ),
        in_specs=[whole] * 11,
        out_specs=(whole, whole, whole),
        scratch_shapes=[
            pltpu.VMEM((far, rows, lanes), BF16),
            pltpu.VMEM((slots, chunks, rows, lanes), F32),
            pltpu.VMEM((slots, chunks, rows, lanes), F32),
            pltpu.VMEM((channels, wide, wide), BF16),
            pltpu.VMEM((rows, wide), F32),
            pltpu.VMEM((rows, wide), F32),
            pltpu.VMEM((chunks, rows, lanes), F32),
            pltpu.VMEM((chunks, rows, lanes), F32),
            pltpu.VMEM((chunks, rows, lanes), F32),
            pltpu.VMEM((far, rows * edge // lanes, lanes), BF16),
            pltpu.VMEM((far, rows * edge // lanes, lanes), BF16),
            pltpu.VMEM((far, rows * edge // lanes, lanes), F32),
            pltpu.VMEM((steps, 6 * channels, channels), F32),
            pltpu.VMEM((steps, 6 * channels, channels), F32),
            pltpu.SemaphoreType.DMA((far,)),
            pltpu.SemaphoreType.DMA((far,)),
            pltpu.SemaphoreType.DMA((far,)),
            pltpu.SemaphoreType.DMA((far,)),
            pltpu.SemaphoreType.DMA((steps,)),
            pltpu.SemaphoreType.DMA((steps,)),
        ],
        compiler_params=pltpu.CompilerParams(
            collective_id=0, has_side_effects=True, vmem_limit_bytes=60 * 1024 * 1024
        ),
    )(own, *slabs, cot, mask, w_in, w_in.T, w_out, w_out.T)
    grad_w_in = weights[: 5 * channels].T
    grad_w_out = weights[5 * channels :]
    return (from_columns(update), from_columns(grad), grad_w_in, grad_w_out)


def solution(mesh):
    tiled = P(("grp", "row"), None, None, None)
    return jax.shard_map(
        local,
        mesh=mesh,
        in_specs=(tiled, P(("grp", "row"), None), P(), P(), tiled),
        out_specs=(tiled, tiled, P("grp", None), P("grp", None)),
        check_vma=False,
    )
```

time: 492 us -> 196 us (0.40); the launches traced: 487 us -> 196 us
  Pallas kernels: 0 us -> 167 us
  waiting for transfers between devices: 138 us -> 0 us
  local copies, waits for them, and re-layouts: 145 us -> 26.1 us
  blocking collectives: 83.3 us -> 0 us
  matrix products: 49.9 us -> 0 us
  other arithmetic: 35.3 us -> 2.47 us
  starting transfers between devices: 19.9 us -> 0 us
  between operations: 15 us -> 0.78 us
    pallas_call x0 -> x1, Pallas kernels: none -> 167 us  [local(): pl.pallas_call(functools.partial(body, devices, slots, edge, channels), o...]
    psum x1 -> x0, waiting for transfers between devices: 90.7 us -> none  [local(): grad_w_in, grad_w_out = lax.psum((grad_in_local, grad_out_local), 'row')]
    psum x1 -> x0, blocking collectives: 83.3 us -> none  [local(): grad_w_in, grad_w_out = lax.psum((grad_in_local, grad_out_local), 'row')]
    dot_general x11 -> x0, local copies, waits for them, and re-layouts: 54.9 us -> none  [the longest x5 24 us: back_product(): jnp.einsum('cij,wcik->wcjk', d_tile, left_part, preferred_element_type=jn...]
    dot_general x21 -> x0, matrix products: 49.9 us -> none  [the longest x5 11.4 us: back_product(): jnp.einsum('cij,wcjk->wcik', d_tile, right_part, preferred_element_type=j...]
    ppermute x8 -> x0, waiting for transfers between devices: 47.7 us -> none  [passed_along(): return lax.ppermute(x, axis, pairs)]
    slice x14 -> x2, local copies, waits for them, and re-layouts: 33 us -> 0.84 us  [the longest x1 0.62 us: local(): grad_w_out = weights[5 * channels:]]
    ppermute x8 -> x0, starting transfers between devices: 19.9 us -> none  [passed_along(): return lax.ppermute(x, axis, pairs)]
  transfers between devices with their start and end apart: 9 -> 0, of which waited for: 3 -> 0; matrix products, arithmetic and copies ran while one was open for 17% -> 0% of each run, Pallas kernels for 0% -> 0%
where the time goes in v2:
time: 196 us
  Pallas kernels  167 us (85%)
  local copies, waits for them, and re-layouts  26.1 us (13%)
  other arithmetic  2.47 us (1%)
    pallas_call x1, Pallas kernels, local(): pl.pallas_call(functools.partial(body, devices, slots, edge, channels), o...  167 us
    another operation x2, local copies, waits for them, and re-layouts, local(): cot = to_columns(cotangent[0].reshape(tiles.shape))  4.22 us
    unnamed x13, local copies, waits for them, and re-layouts  4.13 us

profile of v2, /device:TPU:0, one launch (start us, length us, event | category | flops | bytes accessed | tf_op | source)
XLA Modules:
  0.0 196.1 jit_solution(10138831573775672260)
XLA Ops:
  0.6 0.7 convert_bitcast_fusion
  1.4 0.1 broadcast_in_dim.4
  1.4 0.7 broadcast_in_dim_reshape.3.mask_ref
  2.1 1.4 copy.34
  3.5 1.5 copy.33
  5.0 2.3 %reshape_squeeze.6 = bf16[5,32,32,64]{3,2,1,0:T(8,128)(2,1)S(1)} reshape(bf16[1,5,32,2048]{3,2,1,0:T(8,128)(2,1)} %param.5) | data formatting | bytes 1310720 | tf_op jit(solution)/shard_map/reshape;squeeze | solution.py:312
  7.3 0.4 fusion
  7.7 1.0 reshape.33
  8.7 0.5 copy.35.own_ref
  9.2 0.0 copy-start
  9.2 0.0 copy-start.2
  9.3 0.2 slice.24
  9.5 0.9 pad.8.s3
  10.4 0.4 copy-done.2
  10.8 2.4 %reshape_squeeze.7 = bf16[5,32,32,64]{3,2,1,0:T(8,128)(2,1)} reshape(bf16[1,5,32,2048]{3,2,1,0:T(8,128)(2,1)S(1)} %copy-done.2) | data formatting | bytes 1310720 | tf_op jit(solution)/shard_map/reshape;squeeze | solution.py:314
  13.2 1.8 copy.46
  15.0 1.0 reshape.34
  16.0 0.0 copy-start.4
  16.0 1.3 copy.36.cot_ref
  17.3 1.3 fusion.1
  18.7 166.7 %shard_map.84 = (bf16[2048,160]{1,0:T(8,128)(2,1)}, bf16[2048,160]{1,0:T(8,128)(2,1)}, f32[384,64]{1,0:T(8,128)}) custom-call(bf16[2048,160]{1,0:T(8,128)(2,1)} %copy-done, bf16[2048,128]{1,0:T(8,128)(2,1)} %get-tuple-element.23.s0, bf16[2048,128]{1,0:T(8,128)(2,1)} %get-tuple-element.24.s1, bf16[2048,128]{1,0:T(8,128)(2,1)} %get-tuple-element.22.s2, ...), custom_call_target="tpu_custom_call" | custom-call | tf_op jit(solution)/shard_map/pallas_call | solution.py:326
  185.4 1.5 copy.37
  186.9 0.0 copy-done.3
  186.9 0.6 slice.21
  187.5 0.8 copy.41
  188.3 1.3 reshape.35
  189.6 0.5 copy.38
  190.1 1.8 reshape.36
  192.0 0.5 copy.39
  192.4 1.3 reshape.37
  193.8 0.5 copy.40
  194.3 1.8 reshape.38
  (6 shorter events, 0.0 us)
Async XLA Ops:
  9.2 8.1 %copy-start = (bf16[2048,160]{1,0:T(8,128)(2,1)}, bf16[2048,160]{1,0:T(8,128)(2,1)S(1)}, u32[]{:S(2)}) copy-start(bf16[2048,160]{1,0:T(8,128)(2,1)S(1)} %copy.35.own_ref) | copy-start | bytes 1966084
  9.2 1.6 copy-start.2
  16.0 1.3 copy-start.4
  185.4 1.5 copy-start.3
  190.1 1.8 copy-start.1

commit v3 on v2

--- a/solution.py
+++ b/solution.py
@@ -55,6 +55,16 @@
         ref[(*first, k, rows, slice(None))] = values[:, k * lanes : (k + 1) * lanes]
 
 
+def looped(first, end, batch, compute):
+    def step(block, carry):
+        stores = [compute(block * batch + k) for k in range(batch)]
+        for store in stores:
+            store()
+        return carry
+
+    lax.fori_loop(first // batch, end // batch, step, 0)
+
+
 def body(
     devices,
     slots,
@@ -62,7 +72,7 @@
     channels,
     own_ref, s0, s1, s2, s3, cot_ref, mask_ref, w_in_ref, w_in_t_ref, w_out_ref, w_out_t_ref,
     update_ref, grad_ref, weights_ref,
-    slabs, left, right, band, gates, d_gates, tri, d_left, d_right, packed, arrived, spread,
+    slabs, left, right, band, gates, saved, d_projected, tri, d_left, d_right, packed, arrived, spread,
     terms, landed, slab_send, slab_recv, pack_send, pack_recv, sum_send, sum_recv,
 ):
     half = slots // 2
@@ -137,17 +147,30 @@
     def at(i):
         return pl.ds(pl.multiple_of(i * channels, channels), channels)
 
-    def project_own(i, carry):
+    def four(i):
+        return pl.ds(pl.multiple_of(i * 4 * channels, channels), 4 * channels)
+
+    def project_own(i):
         normed, _ = unit(own_ref[at(i), :].astype(F32))
         projected = dot(w_in_t, normed.astype(BF16), NN)
-        put(left, at(i), gated(projected, channels, 0).astype(BF16).astype(F32), half)
-        put(right, at(i), gated(projected, channels, 1).astype(BF16).astype(F32), half)
-        gates[at(i), :] = jax.nn.sigmoid(projected[4 * channels :])
-        return carry
-
-    lax.fori_loop(0, edge, project_own, 0)
-
-    for d in offsets:
+        parts = []
+        for group in range(2):
+            low = 2 * group * channels
+            parts.append(jax.nn.sigmoid(projected[low : low + channels]))
+            parts.append(projected[low + channels : low + 2 * channels])
+        gate = jax.nn.sigmoid(projected[4 * channels :])
+
+        def store():
+            put(left, at(i), (parts[0] * parts[1]).astype(BF16).astype(F32), half)
+            put(right, at(i), (parts[2] * parts[3]).astype(BF16).astype(F32), half)
+            saved[four(i), :] = jnp.concatenate(parts, axis=0)
+            gates[at(i), :] = gate
+
+        return store
+
+    looped(0, edge, 2, project_own)
+
+    for d in sorted(offsets, key=abs):
         index = offsets.index(d)
         count = slots - abs(d)
         first = max(0, d) * edge
@@ -168,24 +191,34 @@
                 parts = parts + [jnp.zeros((channels, tail), F32)]
             return jnp.concatenate(parts, axis=1)
 
-        def project_far(i, carry, d=d, index=index, placed=placed):
-            normed, _ = unit(slabs[index, at(i), :].astype(F32))
+        def project_far(block, d=d, index=index, placed=placed):
+            picked = [block * 4 + k for k in range(4)]
+            values = jnp.concatenate([slabs[index, at(i), :] for i in picked], axis=1)
+            normed, _ = unit(values.astype(F32))
             projected = dot(w_in_t[: 4 * channels], normed.astype(BF16), NN)
-            for group, ref in enumerate((left, right)):
-                values = placed(gated(projected, channels, group)).astype(BF16).astype(F32)
-                put(ref, at(i), values, half + d)
-            return carry
-
-        lax.fori_loop(0, edge, project_far, 0)
-
-    def triangle(c, carry):
+            results = [gated(projected, channels, group).astype(BF16).astype(F32) for group in range(2)]
+
+            def store():
+                for result, ref in zip(results, (left, right)):
+                    for k, i in enumerate(picked):
+                        put(ref, at(i), placed(result[:, k * lanes : (k + 1) * lanes]), half + d)
+
+            return store
+
+        looped(0, edge // 4, 1, project_far)
+
+    def triangle(c):
         every = pl.ds(c, edge, stride=channels)
         block = jnp.concatenate([taken(right, every, wide, v) for v in range(slots)], axis=0).astype(BF16)
-        band[c] = block
-        put(tri, every, dot(taken(left, every, wide, half).astype(BF16), block, NT))
-        return carry
-
-    lax.fori_loop(0, channels, triangle, 0)
+        result = dot(taken(left, every, wide, half).astype(BF16), block, NT)
+
+        def store():
+            band[c] = block
+            put(tri, every, result)
+
+        return store
+
+    looped(0, channels, 4, triangle)
 
     def middle(start, carry):
         total = carry
@@ -199,7 +232,7 @@
             update_ref[at(i), :] = (mask * gate * mixed).astype(BF16)
             d_update = cot_ref[at(i), :].astype(F32) * mask
             d_mixed = (d_update * gate).astype(BF16)
-            d_gates[at(i), :] = d_update * mixed * gate * (1.0 - gate)
+            d_projected[i, 4 * channels :, :] = (d_update * mixed * gate * (1.0 - gate)).astype(BF16)
             total = total + dot(normed_low, d_mixed, NT)
             d_tri = unit_back(normed, scale, dot(w_out, d_mixed, NN)).astype(BF16).astype(F32)
             put(tri, at(i), d_tri)
@@ -216,12 +249,12 @@
     for d in offsets:
         pl.when(there(d))(lambda d=d: pack_copy(d, -d).start())
 
-    def to_left(c, carry):
+    def to_left(c):
         every = pl.ds(c, edge, stride=channels)
-        put(d_left, every, dot(taken(tri, every, wide).astype(BF16), band[c], NN))
-        return carry
-
-    lax.fori_loop(0, channels, to_left, 0)
+        result = dot(taken(tri, every, wide).astype(BF16), band[c], NN)
+        return lambda: put(d_left, every, result)
+
+    looped(0, channels, 4, to_left)
 
     for d in offsets:
         index = offsets.index(d)
@@ -233,7 +266,7 @@
         pl.when(jnp.logical_not(there(d)))(absent)
         spread[index] = arrived[index].astype(F32)
 
-    def to_right(c, carry):
+    def to_right(c):
         every = pl.ds(c, edge, stride=channels)
         folded = pl.ds(c, edge // folds, stride=channels)
         pieces = []
@@ -248,30 +281,43 @@
                     pieces.append(tile[:, fold * edge : (fold + 1) * edge])
         d_tile = jnp.concatenate(pieces, axis=0).astype(BF16)
         source = jnp.concatenate(sources, axis=0).astype(BF16)
-        put(d_right, every, dot(d_tile, source, TN))
+        result = dot(d_tile, source, TN)
+        return lambda: put(d_right, every, result)
+
+    looped(0, channels, 4, to_right)
+
+    def last(block, carry):
+        stores = []
+        for i in (2 * block, 2 * block + 1):
+            normed, _ = unit(own_ref[at(i), :].astype(F32))
+            held = saved[four(i), :]
+            parts = []
+            for group, ref in enumerate((d_left, d_right)):
+                gate = held[2 * group * channels : (2 * group + 1) * channels]
+                value = held[(2 * group + 1) * channels : (2 * group + 2) * channels]
+                to_value = taken(ref, at(i), wide) * mask * gate
+                parts.append((to_value * value * (1.0 - gate)).astype(BF16))
+                parts.append(to_value.astype(BF16))
+            front = jnp.concatenate(parts, axis=0)
+            stores.append((i, front))
+            joined = jnp.concatenate([front, d_projected[i, 4 * channels :, :]], axis=0)
+            carry = carry + dot(normed.astype(BF16), joined, NT)
+        for i, front in stores:
+            d_projected[i, : 4 * channels, :] = front
         return carry
 
-    lax.fori_loop(0, channels, to_right, 0)
-
-    def last(i, carry):
+    grad_in = lax.fori_loop(0, edge // 2, last, jnp.zeros((channels, 5 * channels), F32))
+
+    def to_pair(i):
         normed, scale = unit(own_ref[at(i), :].astype(F32))
-        normed_low = normed.astype(BF16)
-        projected = dot(w_in_t[: 4 * channels], normed_low, NN)
-        parts = []
-        for group, ref in enumerate((d_left, d_right)):
-            gate = jax.nn.sigmoid(projected[2 * group * channels : (2 * group + 1) * channels])
-            value = projected[(2 * group + 1) * channels : (2 * group + 2) * channels]
-            to_value = taken(ref, at(i), wide) * mask * gate
-            parts.append(to_value * value * (1.0 - gate))
-            parts.append(to_value)
-        parts.append(d_gates[at(i), :])
-        d_projected = jnp.concatenate(parts, axis=0).astype(BF16)
-        grad_ref[at(i), :] = unit_back(normed, scale, dot(w_in, d_projected, NN)).astype(BF16)
-        return carry + dot(d_projected, normed_low, NT)
-
-    grad_in = lax.fori_loop(0, edge, last, jnp.zeros((5 * channels, channels), F32))
-
-    total = jnp.concatenate([grad_in, grad_out], axis=0)
+        result = unit_back(normed, scale, dot(w_in, d_projected[i], NN)).astype(BF16)
+
+        def store():
+            grad_ref[at(i), :] = result
+
+        return store
+
+    total = jnp.concatenate([grad_in, grad_out], axis=1)
     for step, partner in enumerate(partners):
         terms[step] = total
         copy = pltpu.make_async_remote_copy(
@@ -283,6 +329,7 @@
             device_id_type=pl.DeviceIdType.MESH,
         )
         copy.start()
+        looped(edge // 2 * step // steps * 2, edge // 2 * (step + 1) // steps * 2, 2, to_pair)
         copy.wait()
         total = total + landed[step]
     weights_ref[...] = total
@@ -328,7 +375,7 @@
         out_shape=(
             jax.ShapeDtypeStruct((rows, wide), BF16),
             jax.ShapeDtypeStruct((rows, wide), BF16),
-            jax.ShapeDtypeStruct((6 * channels, channels), F32),
+            jax.ShapeDtypeStruct((channels, 6 * channels), F32),
         ),
         in_specs=[whole] * 11,
         out_specs=(whole, whole, whole),
@@ -338,15 +385,16 @@
             pltpu.VMEM((slots, chunks, rows, lanes), F32),
             pltpu.VMEM((channels, wide, wide), BF16),
             pltpu.VMEM((rows, wide), F32),
-            pltpu.VMEM((rows, wide), F32),
+            pltpu.VMEM((4 * rows, wide), F32),
+            pltpu.VMEM((edge, 5 * channels, wide), BF16),
             pltpu.VMEM((chunks, rows, lanes), F32),
             pltpu.VMEM((chunks, rows, lanes), F32),
             pltpu.VMEM((chunks, rows, lanes), F32),
             pltpu.VMEM((far, rows * edge // lanes, lanes), BF16),
             pltpu.VMEM((far, rows * edge // lanes, lanes), BF16),
             pltpu.VMEM((far, rows * edge // lanes, lanes), F32),
-            pltpu.VMEM((steps, 6 * channels, channels), F32),
-            pltpu.VMEM((steps, 6 * channels, channels), F32),
+            pltpu.VMEM((steps, channels, 6 * channels), F32),
+            pltpu.VMEM((steps, channels, 6 * channels), F32),
             pltpu.SemaphoreType.DMA((far,)),
             pltpu.SemaphoreType.DMA((far,)),
             pltpu.SemaphoreType.DMA((far,)),
@@ -355,11 +403,11 @@
             pltpu.SemaphoreType.DMA((steps,)),
         ],
         compiler_params=pltpu.CompilerParams(
-            collective_id=0, has_side_effects=True, vmem_limit_bytes=60 * 1024 * 1024
+            collective_id=0, has_side_effects=True, vmem_limit_bytes=63 * 1024 * 1024
         ),
     )(own, *slabs, cot, mask, w_in, w_in.T, w_out, w_out.T)
-    grad_w_in = weights[: 5 * channels].T
-    grad_w_out = weights[5 * channels :]
+    grad_w_in = weights[:, : 5 * channels]
+    grad_w_out = weights[:, 5 * channels :]
     return (from_columns(update), from_columns(grad), grad_w_in, grad_w_out)
 
 

time: 196 us -> 128 us (0.65)
  Pallas kernels: 167 us -> 97.8 us
    pallas_call x1, Pallas kernels: 167 us -> 97.8 us  [local(): pl.pallas_call(functools.partial(body, devices, slots, edge, channels), o...]
where the time goes in v3:
time: 128 us; the launch traced here: 127 us
  Pallas kernels  97.8 us (76%)
  local copies, waits for them, and re-layouts  26.1 us (20%)
  other arithmetic  2.47 us (2%)
    pallas_call x1, Pallas kernels, local(): pl.pallas_call(functools.partial(body, devices, slots, edge, channels), o...  97.8 us
    another operation x2, local copies, waits for them, and re-layouts, local(): cot = to_columns(cotangent[0].reshape(tiles.shape))  4.22 us
    unnamed x13, local copies, waits for them, and re-layouts  4.01 us
    reshape x4, local copies, waits for them, and re-layouts, to_columns(): return jnp.transpose(tiles, (1, 3, 0, 2)).reshape(rows, wide)  3.75 us
    reshape x2, local copies, waits for them, and re-layouts, from_columns(): return jnp.transpose(tiles, (2, 0, 3, 1)).reshape(pair.shape)  3.63 us
    reshape x2, local copies, waits for them, and re-layouts, from_columns(): tiles = columns.reshape(edge, channels, slots, edge)  2.67 us

profile of v3, /device:TPU:0, one launch (start us, length us, event | category | flops | bytes accessed | tf_op | source)
XLA Modules:
  0.0 127.1 jit_solution(8494783703534784361)
XLA Ops:
  0.6 0.7 convert_bitcast_fusion
  1.4 0.1 broadcast_in_dim.4
  1.4 0.7 broadcast_in_dim_reshape.3.mask_ref
  2.1 1.4 %copy.32 = bf16[64,64]{0,1:T(8,128)(2,1)} copy(bf16[64,64]{1,0:T(8,128)(2,1)} %w_out_ref.1) | data formatting | bytes 16384 | tf_op args[3]
  3.5 1.5 %copy.31 = bf16[64,320]{0,1:T(8,128)(2,1)} copy(bf16[64,320]{1,0:T(8,128)(2,1)} %w_in_ref.1) | data formatting | bytes 81920 | tf_op args[2]
  5.0 2.3 %reshape_squeeze.6 = bf16[5,32,32,64]{3,2,1,0:T(8,128)(2,1)S(1)} reshape(bf16[1,5,32,2048]{3,2,1,0:T(8,128)(2,1)} %param.5) | data formatting | bytes 1310720 | tf_op jit(solution)/shard_map/reshape;squeeze | solution.py:359
  7.3 0.4 fusion
  7.7 1.0 reshape.33
  8.7 0.5 copy.33.own_ref
  9.2 0.0 copy-start
  9.2 0.0 copy-start.2
  9.3 0.2 slice.24
  9.5 0.9 pad.8.s3
  10.4 0.4 copy-done.2
  10.8 2.4 %reshape_squeeze.7 = bf16[5,32,32,64]{3,2,1,0:T(8,128)(2,1)} reshape(bf16[1,5,32,2048]{3,2,1,0:T(8,128)(2,1)S(1)} %copy-done.2) | data formatting | bytes 1310720 | tf_op jit(solution)/shard_map/reshape;squeeze | solution.py:361
  13.2 1.8 %copy.43 = bf16[5,32,32,64]{3,1,2,0:T(8,128)(2,1)S(1)} copy(bf16[5,32,32,64]{3,2,1,0:T(8,128)(2,1)} %reshape_squeeze.7) | data formatting | bytes 1310720 | tf_op jit(solution)/shard_map/reshape;squeeze | solution.py:361
  15.0 1.0 reshape.34
  16.0 0.0 copy-start.4
  16.0 1.3 %copy.34.cot_ref = bf16[2048,160]{1,0:T(8,128)(2,1)} copy(bf16[2048,160]{0,1:T(8,128)(2,1)S(1)} %reshape.34) | data formatting | bytes 1310720 | tf_op jit(solution)/shard_map/reshape | solution.py:353
  17.3 1.3 %fusion.1 = (bf16[2048,128]{1,0:T(8,128)(2,1)}, bf16[2048,128]{1,0:T(8,128)(2,1)}, bf16[2048,128]{1,0:T(8,128)(2,1)}) fusion(bf16[2048,160]{1,0:T(8,128)(2,1)S(1)} %copy.33.own_ref, pred[128]{0:T(512)(128)(4,1)S(1)} %copy-done.4), kind=kLoop, calls=%fused_computation.6 | loop fusion | flops 262144 | bytes 2621568 | tf_op jit(solution)/shard_map/slice | solution.py:368
  18.7 97.8 %shard_map.84 = (bf16[2048,160]{1,0:T(8,128)(2,1)}, bf16[2048,160]{1,0:T(8,128)(2,1)}, f32[64,384]{1,0:T(8,128)}) custom-call(bf16[2048,160]{1,0:T(8,128)(2,1)} %copy-done, bf16[2048,128]{1,0:T(8,128)(2,1)} %get-tuple-element.11.s0, bf16[2048,128]{1,0:T(8,128)(2,1)} %get-tuple-element.12.s1, bf16[2048,128]{1,0:T(8,128)(2,1)} %get-tuple-element.10.s2, ...), custom_call_target="tpu_custom_call" | custom-call | tf_op jit(solution)/shard_map/pallas_call | solution.py:373
  116.5 1.4 %copy.35 = bf16[2048,160]{0,1:T(8,128)(2,1)S(1)} copy(bf16[2048,160]{1,0:T(8,128)(2,1)} %get-tuple-element.7) | data formatting | bytes 1310720 | tf_op jit(solution)/shard_map/pallas_call | solution.py:373
  118.0 0.0 copy-done.3
  118.0 0.7 slice.21
  118.7 1.3 %reshape.35 = bf16[32,64,5,32]{1,0,3,2:T(8,128)(2,1)S(1)} reshape(bf16[2048,160]{0,1:T(8,128)(2,1)S(1)} %copy.35) | data formatting | bytes 1310720 | tf_op jit(solution)/shard_map/reshape | solution.py:356
  120.0 0.5 copy.36
  120.6 1.8 %reshape.36 = bf16[1,5,32,2048]{3,2,1,0:T(8,128)(2,1)} reshape(bf16[5,32,32,64]{3,2,1,0:T(8,128)(2,1)S(1)} %copy.36) | data formatting | bytes 1310720 | tf_op jit(solution)/shard_map/reshape | solution.py:357
  122.4 0.5 copy.37
  122.8 1.3 %reshape.37 = bf16[32,64,5,32]{1,0,3,2:T(8,128)(2,1)S(1)} reshape(bf16[2048,160]{0,1:T(8,128)(2,1)S(1)} %copy.37) | data formatting | bytes 1310720 | tf_op jit(solution)/shard_map/reshape | solution.py:356
  124.2 0.5 copy.38
  124.7 1.8 %reshape.38 = bf16[1,5,32,2048]{3,2,1,0:T(8,128)(2,1)} reshape(bf16[5,32,32,64]{3,2,1,0:T(8,128)(2,1)S(1)} %copy.38) | data formatting | bytes 1310720 | tf_op jit(solution)/shard_map/reshape | solution.py:357
  126.5 0.6 copy.45
  (5 shorter events, 0.0 us)
Async XLA Ops:
  9.2 8.1 %copy-start = (bf16[2048,160]{1,0:T(8,128)(2,1)}, bf16[2048,160]{1,0:T(8,128)(2,1)S(1)}, u32[]{:S(2)}) copy-start(bf16[2048,160]{1,0:T(8,128)(2,1)S(1)} %copy.33.own_ref) | copy-start | bytes 1966084
  9.2 1.6 %copy-start.2 = (bf16[1,5,32,2048]{3,2,1,0:T(8,128)(2,1)S(1)}, bf16[1,5,32,2048]{3,2,1,0:T(8,128)(2,1)}, u32[]{:S(2)}) copy-start(bf16[1,5,32,2048]{3,2,1,0:T(8,128)(2,1)} %param.9) | copy-start | bytes 1966084
  16.0 1.3 %copy-start.4 = (pred[128]{0:T(512)(128)(4,1)S(1)}, pred[128]{0:T(512)(128)(4,1)}, u32[]{:S(2)}) copy-start(pred[128]{0:T(512)(128)(4,1)} %constant.3.clone.1) | copy-start | bytes 388
  116.5 1.5 %copy-start.3 = (f32[64,384]{1,0:T(8,128)S(1)}, f32[64,384]{1,0:T(8,128)}, u32[]{:S(2)}) copy-start(f32[64,384]{1,0:T(8,128)} %get-tuple-element.9) | copy-start | bytes 294916
  120.5 1.8 %copy-start.1 = (bf16[2048,160]{1,0:T(8,128)(2,1)S(1)}, bf16[2048,160]{1,0:T(8,128)(2,1)}, u32[]{:S(2)}) copy-start(bf16[2048,160]{1,0:T(8,128)(2,1)} %get-tuple-element.8) | copy-start | bytes 1966084

commit v4 on v3

--- a/solution.py
+++ b/solution.py
@@ -70,7 +70,7 @@
     slots,
     edge,
     channels,
-    own_ref, s0, s1, s2, s3, cot_ref, mask_ref, w_in_ref, w_in_t_ref, w_out_ref, w_out_t_ref,
+    own_ref, low_ref, high_ref, cot_ref, mask_ref, w_in_ref, w_in_t_ref, w_out_ref, w_out_t_ref,
     update_ref, grad_ref, weights_ref,
     slabs, left, right, band, gates, saved, d_projected, tri, d_left, d_right, packed, arrived, spread,
     terms, landed, slab_send, slab_recv, pack_send, pack_recv, sum_send, sum_recv,
@@ -82,7 +82,6 @@
     folds = lanes // edge
     steps = devices.bit_length() - 1
     offsets = [d for d in range(-half, half + 1) if d != 0]
-    slab_refs = dict(zip(offsets, (s0, s1, s2, s3)))
     me = lax.axis_index("row")
 
     def there(d):
@@ -105,25 +104,32 @@
         greet(partner)
     pl.semaphore_wait(barrier, steps + sum(there(d).astype(jnp.int32) for d in offsets))
 
-    def slab_copy(d):
+    even = lax.rem(me, 2) == 0
+    odd = jnp.logical_not(even)
+
+    def slab_copy(source, sem, target, landing):
         return pltpu.make_async_remote_copy(
-            src_ref=slab_refs[d],
-            dst_ref=slabs.at[offsets.index(-d)],
-            send_sem=slab_send.at[offsets.index(d)],
-            recv_sem=slab_recv.at[offsets.index(-d)],
-            device_id={"row": me + d},
+            src_ref=source,
+            dst_ref=slabs.at[offsets.index(landing)],
+            send_sem=slab_send.at[sem],
+            recv_sem=slab_recv.at[offsets.index(landing)],
+            device_id={"row": me + target},
             device_id_type=pl.DeviceIdType.MESH,
         )
 
-    def slab_arrival(d):
-        return pltpu.make_async_remote_copy(
-            src_ref=slab_refs[d],
-            dst_ref=slabs.at[offsets.index(d)],
-            send_sem=slab_send.at[offsets.index(d)],
-            recv_sem=slab_recv.at[offsets.index(d)],
-            device_id={"row": me + d},
-            device_id_type=pl.DeviceIdType.MESH,
-        )
+    sends = [
+        (there(1), slab_copy(high_ref, 0, 1, -1)),
+        (there(-1), slab_copy(low_ref, 1, -1, 1)),
+        (jnp.logical_and(even, there(2)), slab_copy(high_ref, 2, 2, -2)),
+        (jnp.logical_and(odd, there(-2)), slab_copy(low_ref, 3, -2, 2)),
+    ]
+    relays = [
+        (
+            jnp.logical_and(even, jnp.logical_and(there(-1), there(1))),
+            slab_copy(slabs.at[offsets.index(-1)], 4, 1, -2),
+        ),
+        (jnp.logical_and(odd, there(1)), slab_copy(slabs.at[offsets.index(1)], 5, -1, 2)),
+    ]
 
     def pack_copy(d, landing):
         return pltpu.make_async_remote_copy(
@@ -135,8 +141,8 @@
             device_id_type=pl.DeviceIdType.MESH,
         )
 
-    for d in offsets:
-        pl.when(there(d))(lambda d=d: slab_copy(d).start())
+    for needed, copy in sends:
+        pl.when(needed)(copy.start)
 
     w_in = w_in_ref[...]
     w_in_t = w_in_t_ref[...]
@@ -170,28 +176,30 @@
 
     looped(0, edge, 2, project_own)
 
-    for d in sorted(offsets, key=abs):
+    def project_slab(d, relay):
         index = offsets.index(d)
-        count = slots - abs(d)
+        count = (slots - abs(d)) * edge
+        skipped = max(0, -d - 1) * edge
         first = max(0, d) * edge
 
-        def absent(index=index):
+        def absent():
             slabs[index] = jnp.zeros((rows, lanes), BF16)
 
-        pl.when(there(d))(lambda d=d: slab_arrival(d).wait_recv())
+        pl.when(there(d))(lambda: slab_copy(low_ref, 0, d, d).wait_recv())
         pl.when(jnp.logical_not(there(d)))(absent)
-
-        def placed(values, first=first, count=count):
-            values = values[:, : count * edge]
-            parts = [values]
+        if relay is not None:
+            pl.when(relay[0])(relay[1].start)
+
+        def placed(values):
+            parts = [values[:, skipped : skipped + count]]
             if first > 0:
                 parts = [jnp.zeros((channels, first), F32)] + parts
-            tail = wide - first - count * edge
+            tail = wide - first - count
             if tail > 0:
                 parts = parts + [jnp.zeros((channels, tail), F32)]
             return jnp.concatenate(parts, axis=1)
 
-        def project_far(block, d=d, index=index, placed=placed):
+        def project_far(block):
             picked = [block * 4 + k for k in range(4)]
             values = jnp.concatenate([slabs[index, at(i), :] for i in picked], axis=1)
             normed, _ = unit(values.astype(F32))
@@ -206,6 +214,13 @@
             return store
 
         looped(0, edge // 4, 1, project_far)
+
+    pl.when(even)(lambda: project_slab(1, None))
+    pl.when(odd)(lambda: project_slab(-1, None))
+    pl.when(even)(lambda: project_slab(-1, relays[0]))
+    pl.when(odd)(lambda: project_slab(1, relays[1]))
+    project_slab(-2, None)
+    project_slab(2, None)
 
     def triangle(c):
         every = pl.ds(c, edge, stride=channels)
@@ -256,15 +271,57 @@
 
     looped(0, channels, 4, to_left)
 
-    for d in offsets:
-        index = offsets.index(d)
-
-        def absent(index=index):
-            arrived[index] = jnp.zeros(arrived.shape[1:], BF16)
-
-        pl.when(there(d))(lambda d=d: pack_copy(d, d).wait_recv())
-        pl.when(jnp.logical_not(there(d)))(absent)
-        spread[index] = arrived[index].astype(F32)
+    def weigh(group, ref, joined_gate):
+        def compute(block, carry):
+            stores = []
+            for i in (2 * block, 2 * block + 1):
+                normed, _ = unit(own_ref[at(i), :].astype(F32))
+                held = saved[four(i), :]
+                gate = held[2 * group * channels : (2 * group + 1) * channels]
+                value = held[(2 * group + 1) * channels : (2 * group + 2) * channels]
+                to_value = taken(ref, at(i), wide) * mask * gate
+                front = jnp.concatenate([to_value * value * (1.0 - gate), to_value], axis=0).astype(BF16)
+                stores.append((i, front))
+                if joined_gate:
+                    front = jnp.concatenate([front, d_projected[i, 4 * channels :, :]], axis=0)
+                carry = carry + dot(normed.astype(BF16), front, NT)
+            for i, front in stores:
+                d_projected[i, 2 * group * channels : (2 * group + 2) * channels, :] = front
+            return carry
+
+        width = (3 if joined_gate else 2) * channels
+        return lax.fori_loop(0, edge // 2, compute, jnp.zeros((channels, width), F32))
+
+    def summed(total, first, sem, beside):
+        width = total.shape[1]
+        for step, partner in enumerate(partners):
+            terms[step, :, first : first + width] = total
+            copy = pltpu.make_async_remote_copy(
+                src_ref=terms.at[step, :, pl.ds(first, width)],
+                dst_ref=landed.at[step, :, pl.ds(first, width)],
+                send_sem=sum_send.at[sem + step],
+                recv_sem=sum_recv.at[sem + step],
+                device_id={"row": partner},
+                device_id_type=pl.DeviceIdType.MESH,
+            )
+            copy.start()
+            beside(step)
+            copy.wait()
+            total = total + landed[step, :, first : first + width]
+        weights_ref[:, first : first + width] = total
+
+    early = jnp.concatenate([weigh(0, d_left, True), grad_out], axis=1)
+
+    def take_packs():
+        for d in offsets:
+            index = offsets.index(d)
+
+            def absent(index=index):
+                arrived[index] = jnp.zeros(arrived.shape[1:], BF16)
+
+            pl.when(there(d))(lambda d=d: pack_copy(d, d).wait_recv())
+            pl.when(jnp.logical_not(there(d)))(absent)
+            spread[index] = arrived[index].astype(F32)
 
     def to_right(c):
         every = pl.ds(c, edge, stride=channels)
@@ -284,29 +341,13 @@
         result = dot(d_tile, source, TN)
         return lambda: put(d_right, every, result)
 
-    looped(0, channels, 4, to_right)
-
-    def last(block, carry):
-        stores = []
-        for i in (2 * block, 2 * block + 1):
-            normed, _ = unit(own_ref[at(i), :].astype(F32))
-            held = saved[four(i), :]
-            parts = []
-            for group, ref in enumerate((d_left, d_right)):
-                gate = held[2 * group * channels : (2 * group + 1) * channels]
-                value = held[(2 * group + 1) * channels : (2 * group + 2) * channels]
-                to_value = taken(ref, at(i), wide) * mask * gate
-                parts.append((to_value * value * (1.0 - gate)).astype(BF16))
-                parts.append(to_value.astype(BF16))
-            front = jnp.concatenate(parts, axis=0)
-            stores.append((i, front))
-            joined = jnp.concatenate([front, d_projected[i, 4 * channels :, :]], axis=0)
-            carry = carry + dot(normed.astype(BF16), joined, NT)
-        for i, front in stores:
-            d_projected[i, : 4 * channels, :] = front
-        return carry
-
-    grad_in = lax.fori_loop(0, edge // 2, last, jnp.zeros((channels, 5 * channels), F32))
+    def beside_early(step):
+        if step == 0:
+            take_packs()
+        looped(channels // 4 * step // steps * 4, channels // 4 * (step + 1) // steps * 4, 4, to_right)
+
+    summed(early, 0, 0, beside_early)
+    late = weigh(1, d_right, False)
 
     def to_pair(i):
         normed, scale = unit(own_ref[at(i), :].astype(F32))
@@ -317,25 +358,14 @@
 
         return store
 
-    total = jnp.concatenate([grad_in, grad_out], axis=1)
-    for step, partner in enumerate(partners):
-        terms[step] = total
-        copy = pltpu.make_async_remote_copy(
-            src_ref=terms.at[step],
-            dst_ref=landed.at[step],
-            send_sem=sum_send.at[step],
-            recv_sem=sum_recv.at[step],
-            device_id={"row": partner},
-            device_id_type=pl.DeviceIdType.MESH,
-        )
-        copy.start()
+    def beside_late(step):
         looped(edge // 2 * step // steps * 2, edge // 2 * (step + 1) // steps * 2, 2, to_pair)
-        copy.wait()
-        total = total + landed[step]
-    weights_ref[...] = total
-
+
+    summed(late, 4 * channels, steps, beside_late)
+
+    for needed, copy in sends + relays:
+        pl.when(needed)(copy.wait_send)
     for d in offsets:
-        pl.when(there(d))(lambda d=d: slab_copy(d).wait_send())
         pl.when(there(d))(lambda d=d: pack_copy(d, -d).wait_send())
 
 
@@ -344,7 +374,7 @@
     channels = w_in.shape[0]
     half = slots // 2
     rows, wide = edge * channels, slots * edge
-    lanes = 128
+    lanes = wide - edge
     chunks = -(-wide // lanes)
     devices = lax.axis_size("row")
     steps = devices.bit_length() - 1
@@ -360,16 +390,10 @@
     own = to_columns(tiles * kept[0].astype(BF16)[:, None, None, None])
     cot = to_columns(cotangent[0].reshape(tiles.shape))
     mask = jnp.repeat(kept[0].astype(F32), edge)[None, :]
-    slabs = []
-    for d in range(-half, half + 1):
-        if d != 0:
-            low = max(0, d) * edge
-            count = (slots - abs(d)) * edge
-            slab = own[:, low : low + count]
-            slabs.append(jnp.pad(slab, ((0, 0), (0, lanes - count))))
+    low, high = own[:, :lanes], own[:, edge:]
 
     whole = pl.BlockSpec(memory_space=pltpu.VMEM)
-    far = len(slabs)
+    far = 2 * half
     update, grad, weights = pl.pallas_call(
         functools.partial(body, devices, slots, edge, channels),
         out_shape=(
@@ -377,7 +401,7 @@
             jax.ShapeDtypeStruct((rows, wide), BF16),
             jax.ShapeDtypeStruct((channels, 6 * channels), F32),
         ),
-        in_specs=[whole] * 11,
+        in_specs=[whole] * 9,
         out_specs=(whole, whole, whole),
         scratch_shapes=[
             pltpu.VMEM((far, rows, lanes), BF16),
@@ -395,19 +419,22 @@
             pltpu.VMEM((far, rows * edge // lanes, lanes), F32),
             pltpu.VMEM((steps, channels, 6 * channels), F32),
             pltpu.VMEM((steps, channels, 6 * channels), F32),
+            pltpu.SemaphoreType.DMA((far + 2,)),
             pltpu.SemaphoreType.DMA((far,)),
             pltpu.SemaphoreType.DMA((far,)),
             pltpu.SemaphoreType.DMA((far,)),
-            pltpu.SemaphoreType.DMA((far,)),
-            pltpu.SemaphoreType.DMA((steps,)),
-            pltpu.SemaphoreType.DMA((steps,)),
+            pltpu.SemaphoreType.DMA((2 * steps,)),
+            pltpu.SemaphoreType.DMA((2 * steps,)),
         ],
         compiler_params=pltpu.CompilerParams(
             collective_id=0, has_side_effects=True, vmem_limit_bytes=63 * 1024 * 1024
         ),
-    )(own, *slabs, cot, mask, w_in, w_in.T, w_out, w_out.T)
-    grad_w_in = weights[:, : 5 * channels]
-    grad_w_out = weights[:, 5 * channels :]
+    )(own, low, high, cot, mask, w_in, w_in.T, w_out, w_out.T)
+    first, gate, out, second = jnp.split(
+        weights, [2 * channels, 3 * channels, 4 * channels], axis=1
+    )
+    grad_w_in = jnp.concatenate([first, second, gate], axis=1)
+    grad_w_out = out
     return (from_columns(update), from_columns(grad), grad_w_in, grad_w_out)
 
 

time: 128 us -> 115 us (0.90)
  Pallas kernels: 97.8 us -> 87 us
    pallas_call x1, Pallas kernels: 97.8 us -> 87 us  [local(): pl.pallas_call(functools.partial(body, devices, slots, edge, channels), o...]
    slice x1 -> x0, other arithmetic: 1.34 us -> none  [local(): slab = own[:, low:low + count]]
    unnamed x13 -> x10, local copies, waits for them, and re-layouts: 4.01 us -> 3.29 us
where the time goes in v4:
time: 115 us
  Pallas kernels  87 us (76%)
  local copies, waits for them, and re-layouts  25.5 us (22%)
  other arithmetic  1.78 us (2%)
    pallas_call x1, Pallas kernels, local(): pl.pallas_call(functools.partial(body, devices, slots, edge, channels), o...  87 us
    another operation x2, local copies, waits for them, and re-layouts, local(): cot = to_columns(cotangent[0].reshape(tiles.shape))  4.25 us
    reshape x4, local copies, waits for them, and re-layouts, to_columns(): return jnp.transpose(tiles, (1, 3, 0, 2)).reshape(rows, wide)  3.75 us
    reshape x2, local copies, waits for them, and re-layouts, from_columns(): return jnp.transpose(tiles, (2, 0, 3, 1)).reshape(pair.shape)  3.63 us
    unnamed x10, local copies, waits for them, and re-layouts  3.29 us
    reshape x2, local copies, waits for them, and re-layouts, from_columns(): tiles = columns.reshape(edge, channels, slots, edge)  2.67 us
    another operation x1, local copies, waits for them, and re-layouts, local(): tiles = pair[0].reshape(slots, edge, edge, channels)  2.3 us

profile of v4, /device:TPU:0, one launch (start us, length us, event | category | flops | bytes accessed | tf_op | source)
XLA Modules:
  0.0 115.0 jit_solution(647347746436777616)
XLA Ops:
  0.6 0.7 convert_bitcast_fusion
  1.4 0.1 broadcast_in_dim.4
  1.4 0.6 broadcast_in_dim_reshape.3.mask_ref
  2.1 1.4 %copy.30 = bf16[64,64]{0,1:T(8,128)(2,1)} copy(bf16[64,64]{1,0:T(8,128)(2,1)} %w_out_ref.1) | data formatting | bytes 16384 | tf_op args[3]
  3.5 1.5 %copy.29 = bf16[64,320]{0,1:T(8,128)(2,1)} copy(bf16[64,320]{1,0:T(8,128)(2,1)} %w_in_ref.1) | data formatting | bytes 81920 | tf_op args[2]
  5.0 2.3 %reshape_squeeze.6 = bf16[5,32,32,64]{3,2,1,0:T(8,128)(2,1)S(1)} reshape(bf16[1,5,32,2048]{3,2,1,0:T(8,128)(2,1)} %param.5) | data formatting | bytes 1310720 | tf_op jit(solution)/shard_map/reshape;squeeze | solution.py:389
  7.3 0.4 fusion
  7.7 1.0 reshape.33
  8.7 0.5 copy.31.own_ref
  9.2 0.0 copy-start
  9.2 0.0 copy-start.2
  9.2 1.2 %fusion.1 = (bf16[2048,128]{1,0:T(8,128)(2,1)}, bf16[2048,128]{1,0:T(8,128)(2,1)}) fusion(bf16[2048,160]{1,0:T(8,128)(2,1)S(1)} %copy.31.own_ref), kind=kLoop, calls=%fused_computation.6 | loop fusion | bytes 2097152 | tf_op jit(solution)/shard_map/slice | solution.py:393
  10.5 0.3 copy-done.2
  10.8 2.4 %reshape_squeeze.7 = bf16[5,32,32,64]{3,2,1,0:T(8,128)(2,1)} reshape(bf16[1,5,32,2048]{3,2,1,0:T(8,128)(2,1)S(1)} %copy-done.2) | data formatting | bytes 1310720 | tf_op jit(solution)/shard_map/reshape;squeeze | solution.py:391
  13.2 0.0 copy-done
  13.2 1.8 %copy.41 = bf16[5,32,32,64]{3,1,2,0:T(8,128)(2,1)S(1)} copy(bf16[5,32,32,64]{3,2,1,0:T(8,128)(2,1)} %reshape_squeeze.7) | data formatting | bytes 1310720 | tf_op jit(solution)/shard_map/reshape;squeeze | solution.py:391
  15.1 1.0 reshape.34
  16.0 1.3 %copy.32.cot_ref = bf16[2048,160]{1,0:T(8,128)(2,1)} copy(bf16[2048,160]{0,1:T(8,128)(2,1)S(1)} %reshape.34) | data formatting | bytes 1310720 | tf_op jit(solution)/shard_map/reshape | solution.py:383
  17.3 87.0 %shard_map.84 = (bf16[2048,160]{1,0:T(8,128)(2,1)}, bf16[2048,160]{1,0:T(8,128)(2,1)}, f32[64,384]{1,0:T(8,128)}) custom-call(bf16[2048,160]{1,0:T(8,128)(2,1)} %copy-done, bf16[2048,128]{1,0:T(8,128)(2,1)} %get-tuple-element.11.low_ref, bf16[2048,128]{1,0:T(8,128)(2,1)} %get-tuple-element.10.high_ref, bf16[2048,160]{1,0:T(8,128)(2,1)} %copy.32.cot_ref, ...), custom_call_target="tpu_custom_call" | custom-call | tf_op jit(solution)/shard_map/pallas_call | solution.py:397
  104.3 0.0 copy-start.3
  104.3 1.4 %copy.33 = bf16[2048,160]{0,1:T(8,128)(2,1)S(1)} copy(bf16[2048,160]{1,0:T(8,128)(2,1)} %get-tuple-element.7) | data formatting | bytes 1310720 | tf_op jit(solution)/shard_map/pallas_call | solution.py:397
  105.8 0.0 copy-done.3
  105.8 0.7 fusion.2
  106.5 0.6 pad_maximum_fusion
  107.2 1.3 %reshape.35 = bf16[32,64,5,32]{1,0,3,2:T(8,128)(2,1)S(1)} reshape(bf16[2048,160]{0,1:T(8,128)(2,1)S(1)} %copy.33) | data formatting | bytes 1310720 | tf_op jit(solution)/shard_map/reshape | solution.py:386
  108.5 0.5 copy.34
  109.0 0.0 copy-start.1
  109.0 1.8 %reshape.36 = bf16[1,5,32,2048]{3,2,1,0:T(8,128)(2,1)} reshape(bf16[5,32,32,64]{3,2,1,0:T(8,128)(2,1)S(1)} %copy.34) | data formatting | bytes 1310720 | tf_op jit(solution)/shard_map/reshape | solution.py:387
  110.9 0.5 copy.35
  111.3 1.3 %reshape.37 = bf16[32,64,5,32]{1,0,3,2:T(8,128)(2,1)S(1)} reshape(bf16[2048,160]{0,1:T(8,128)(2,1)S(1)} %copy.35) | data formatting | bytes 1310720 | tf_op jit(solution)/shard_map/reshape | solution.py:386
  112.7 0.5 copy.36
  113.2 1.8 %reshape.38 = bf16[1,5,32,2048]{3,2,1,0:T(8,128)(2,1)} reshape(bf16[5,32,32,64]{3,2,1,0:T(8,128)(2,1)S(1)} %copy.36) | data formatting | bytes 1310720 | tf_op jit(solution)/shard_map/reshape | solution.py:387
  (2 shorter events, 0.0 us)
Async XLA Ops:
  9.2 4.0 %copy-start = (bf16[2048,160]{1,0:T(8,128)(2,1)}, bf16[2048,160]{1,0:T(8,128)(2,1)S(1)}, u32[]{:S(2)}) copy-start(bf16[2048,160]{1,0:T(8,128)(2,1)S(1)} %copy.31.own_ref) | copy-start | bytes 1966084
  9.2 1.6 %copy-start.2 = (bf16[1,5,32,2048]{3,2,1,0:T(8,128)(2,1)S(1)}, bf16[1,5,32,2048]{3,2,1,0:T(8,128)(2,1)}, u32[]{:S(2)}) copy-start(bf16[1,5,32,2048]{3,2,1,0:T(8,128)(2,1)} %param.9) | copy-start | bytes 1966084
  104.3 1.5 %copy-start.3 = (f32[64,384]{1,0:T(8,128)S(1)}, f32[64,384]{1,0:T(8,128)}, u32[]{:S(2)}) copy-start(f32[64,384]{1,0:T(8,128)} %get-tuple-element.9) | copy-start | bytes 294916
  109.0 1.8 %copy-start.1 = (bf16[2048,160]{1,0:T(8,128)(2,1)S(1)}, bf16[2048,160]{1,0:T(8,128)(2,1)}, u32[]{:S(2)}) copy-start(bf16[2048,160]{1,0:T(8,128)(2,1)} %get-tuple-element.8) | copy-start | bytes 1966084

commit v5 on v4

--- a/solution.py
+++ b/solution.py
@@ -170,7 +170,7 @@
             put(left, at(i), (parts[0] * parts[1]).astype(BF16).astype(F32), half)
             put(right, at(i), (parts[2] * parts[3]).astype(BF16).astype(F32), half)
             saved[four(i), :] = jnp.concatenate(parts, axis=0)
-            gates[at(i), :] = gate
+            put(gates, at(i), gate)
 
         return store
 
@@ -217,6 +217,22 @@
 
     pl.when(even)(lambda: project_slab(1, None))
     pl.when(odd)(lambda: project_slab(-1, None))
+
+    def piece(block):
+        return pl.ds(pl.multiple_of(block * 128, 128), 128)
+
+    def cot_to_rows(block):
+        values = cot_ref[:, piece(block)].astype(F32).T
+        return lambda: put(d_left, piece(block), values)
+
+    def cot_to_blocks(c):
+        every = pl.ds(c, edge, stride=channels)
+        turned = taken(d_left, every, wide).T
+        values = jnp.concatenate([turned[w * edge : (w + 1) * edge] for w in range(slots)], axis=1)
+        return lambda: put(d_right, every, values)
+
+    looped(0, rows // 128, 2, cot_to_rows)
+    looped(0, channels, 4, cot_to_blocks)
     pl.when(even)(lambda: project_slab(-1, relays[0]))
     pl.when(odd)(lambda: project_slab(1, relays[1]))
     project_slab(-2, None)
@@ -243,9 +259,9 @@
             normed, scale = unit(taken(tri, at(i), wide))
             normed_low = normed.astype(BF16)
             mixed = dot(w_out_t, normed_low, NN)
-            gate = gates[at(i), :]
-            update_ref[at(i), :] = (mask * gate * mixed).astype(BF16)
-            d_update = cot_ref[at(i), :].astype(F32) * mask
+            gate = taken(gates, at(i), wide)
+            put(gates, at(i), mask * gate * mixed)
+            d_update = taken(d_right, at(i), wide) * mask
             d_mixed = (d_update * gate).astype(BF16)
             d_projected[i, 4 * channels :, :] = (d_update * mixed * gate * (1.0 - gate)).astype(BF16)
             total = total + dot(normed_low, d_mixed, NT)
@@ -358,7 +374,28 @@
 
         return store
 
+    def update_to_rows(c):
+        every = pl.ds(c, edge, stride=channels)
+        values = taken(gates, every, wide)
+        values = jnp.concatenate([values[:, w * edge : (w + 1) * edge] for w in range(slots)], axis=0).T
+        return lambda: put(tri, every, values)
+
+    def update_to_tiles(block):
+        values = taken(tri, piece(block), wide).T.astype(BF16)
+
+        def store():
+            update_ref[:, piece(block)] = values
+
+        return store
+
     def beside_late(step):
+        middle_step = steps // 2
+        if step < middle_step:
+            blocks = channels // 4
+            looped(blocks * step // middle_step * 4, blocks * (step + 1) // middle_step * 4, 4, update_to_rows)
+        else:
+            blocks, step_now, step_count = rows // 256, step - middle_step, steps - middle_step
+            looped(blocks * step_now // step_count * 2, blocks * (step_now + 1) // step_count * 2, 2, update_to_tiles)
         looped(edge // 2 * step // steps * 2, edge // 2 * (step + 1) // steps * 2, 2, to_pair)
 
     summed(late, 4 * channels, steps, beside_late)
@@ -388,7 +425,7 @@
 
     tiles = pair[0].reshape(slots, edge, edge, channels)
     own = to_columns(tiles * kept[0].astype(BF16)[:, None, None, None])
-    cot = to_columns(cotangent[0].reshape(tiles.shape))
+    cot = cotangent[0].reshape(wide, rows)
     mask = jnp.repeat(kept[0].astype(F32), edge)[None, :]
     low, high = own[:, :lanes], own[:, edge:]
 
@@ -397,7 +434,7 @@
     update, grad, weights = pl.pallas_call(
         functools.partial(body, devices, slots, edge, channels),
         out_shape=(
-            jax.ShapeDtypeStruct((rows, wide), BF16),
+            jax.ShapeDtypeStruct((wide, rows), BF16),
             jax.ShapeDtypeStruct((rows, wide), BF16),
             jax.ShapeDtypeStruct((channels, 6 * channels), F32),
         ),
@@ -408,7 +445,7 @@
             pltpu.VMEM((slots, chunks, rows, lanes), F32),
             pltpu.VMEM((slots, chunks, rows, lanes), F32),
             pltpu.VMEM((channels, wide, wide), BF16),
-            pltpu.VMEM((rows, wide), F32),
+            pltpu.VMEM((chunks, rows, lanes), F32),
             pltpu.VMEM((4 * rows, wide), F32),
             pltpu.VMEM((edge, 5 * channels, wide), BF16),
             pltpu.VMEM((chunks, rows, lanes), F32),
@@ -435,7 +472,7 @@
     )
     grad_w_in = jnp.concatenate([first, second, gate], axis=1)
     grad_w_out = out
-    return (from_columns(update), from_columns(grad), grad_w_in, grad_w_out)
+    return (update.reshape(pair.shape), from_columns(grad), grad_w_in, grad_w_out)
 
 
 def solution(mesh):

time: 115 us -> 111 us (0.965)
  local copies, waits for them, and re-layouts: 25.5 us -> 17.8 us
  Pallas kernels: 87 us -> 90 us
    another operation x2 -> x0, local copies, waits for them, and re-layouts: 4.25 us -> none  [local(): cot = to_columns(cotangent[0].reshape(tiles.shape))]
    pallas_call x1, Pallas kernels: 87 us -> 90 us  [local(): pl.pallas_call(functools.partial(body, devices, slots, edge, channels), o...]
    reshape x4 -> x2, local copies, waits for them, and re-layouts: 3.75 us -> 1.48 us  [to_columns(): return jnp.transpose(tiles, (1, 3, 0, 2)).reshape(rows, wide)]
    reshape x2 -> x1, local copies, waits for them, and re-layouts: 3.63 us -> 1.82 us  [from_columns(): return jnp.transpose(tiles, (2, 0, 3, 1)).reshape(pair.shape)]
    split x2, local copies, waits for them, and re-layouts: 0.7 us -> 2.31 us  [local(): jnp.split(weights, [2 * channels, 3 * channels, 4 * channels], axis=1)]
    unnamed x10 -> x7, local copies, waits for them, and re-layouts: 3.29 us -> 4.75 us
    reshape x2 -> x1, local copies, waits for them, and re-layouts: 2.67 us -> 1.34 us  [from_columns(): tiles = columns.reshape(edge, channels, slots, edge)]
where the time goes in v5:
time: 111 us; the launch traced here: 110 us
  Pallas kernels  90 us (81%)
  local copies, waits for them, and re-layouts  17.8 us (16%)
  other arithmetic  1.78 us (2%)
    pallas_call x1, Pallas kernels, local(): pl.pallas_call(functools.partial(body, devices, slots, edge, channels), o...  90 us
    unnamed x7, local copies, waits for them, and re-layouts  4.75 us
    split x2, local copies, waits for them, and re-layouts, local(): jnp.split(weights, [2 * channels, 3 * channels, 4 * channels], axis=1)  2.31 us
    another operation x1, local copies, waits for them, and re-layouts, local(): tiles = pair[0].reshape(slots, edge, edge, channels)  2.3 us

profile of v5, /device:TPU:0, one launch (start us, length us, event | category | flops | bytes accessed | tf_op | source)
XLA Modules:
  0.0 110.2 jit_solution(2288770684810582229)
XLA Ops:
  0.6 0.7 convert_bitcast_fusion
  1.4 0.1 broadcast_in_dim.4
  1.4 0.6 broadcast_in_dim_reshape.3.mask_ref
  2.1 1.4 %copy.24 = bf16[64,64]{0,1:T(8,128)(2,1)} copy(bf16[64,64]{1,0:T(8,128)(2,1)} %w_out_ref.1) | data formatting | bytes 16384 | tf_op args[3]
  3.5 1.5 %copy.23 = bf16[64,320]{0,1:T(8,128)(2,1)} copy(bf16[64,320]{1,0:T(8,128)(2,1)} %w_in_ref.1) | data formatting | bytes 81920 | tf_op args[2]
  5.0 2.3 %reshape_squeeze.6 = bf16[5,32,32,64]{3,2,1,0:T(8,128)(2,1)S(1)} reshape(bf16[1,5,32,2048]{3,2,1,0:T(8,128)(2,1)} %param.5) | data formatting | bytes 1310720 | tf_op jit(solution)/shard_map/reshape;squeeze | solution.py:426
  7.3 0.4 fusion
  7.7 1.0 reshape.27
  8.7 0.5 copy.25.own_ref
  9.2 0.0 copy-start
  9.2 1.0 copy-done
  10.2 1.2 %fusion.1 = (bf16[2048,128]{1,0:T(8,128)(2,1)}, bf16[2048,128]{1,0:T(8,128)(2,1)}) fusion(bf16[2048,160]{1,0:T(8,128)(2,1)S(1)} %copy.25.own_ref), kind=kLoop, calls=%fused_computation.5 | loop fusion | bytes 2097152 | tf_op jit(solution)/shard_map/slice | solution.py:430
  11.4 90.0 %shard_map.84 = (bf16[160,2048]{1,0:T(8,128)(2,1)}, bf16[2048,160]{1,0:T(8,128)(2,1)}, f32[64,384]{1,0:T(8,128)}) custom-call(bf16[2048,160]{1,0:T(8,128)(2,1)} %copy-done, bf16[2048,128]{1,0:T(8,128)(2,1)} %get-tuple-element.11.low_ref, bf16[2048,128]{1,0:T(8,128)(2,1)} %get-tuple-element.10.high_ref, bf16[160,2048]{1,0:T(8,128)(2,1)} %bitcast.23, ...), custom_call_target="tpu_custom_call" | custom-call | tf_op jit(solution)/shard_map/pallas_call | solution.py:434
  101.3 1.5 %fusion.2 = (f32[64,64]{1,0:T(8,128)}, f32[64,64]{1,0:T(8,128)S(1)}) fusion(f32[64,384]{1,0:T(8,128)} %get-tuple-element.9), kind=kLoop, calls=%fused_computation.6 | loop fusion | bytes 65536 | tf_op jit(solution)/shard_map/split | solution.py:470
  102.9 0.8 fusion.3
  103.7 0.6 pad_maximum_fusion
  104.3 1.4 %copy.26 = bf16[2048,160]{0,1:T(8,128)(2,1)S(1)} copy(bf16[2048,160]{1,0:T(8,128)(2,1)} %get-tuple-element.8) | data formatting | bytes 1310720 | tf_op jit(solution)/shard_map/pallas_call | solution.py:434
  105.7 1.3 %reshape.29 = bf16[32,64,5,32]{1,0,3,2:T(8,128)(2,1)S(1)} reshape(bf16[2048,160]{0,1:T(8,128)(2,1)S(1)} %copy.26) | data formatting | bytes 1310720 | tf_op jit(solution)/shard_map/reshape | solution.py:423
  107.1 0.5 copy.27
  107.6 0.0 copy-start.1
  107.6 1.8 %reshape.30 = bf16[1,5,32,2048]{3,2,1,0:T(8,128)(2,1)} reshape(bf16[5,32,32,64]{3,2,1,0:T(8,128)(2,1)S(1)} %copy.27) | data formatting | bytes 1310720 | tf_op jit(solution)/shard_map/reshape | solution.py:424
  109.4 0.0 copy-done.1
  109.4 0.8 copy.32
Async XLA Ops:
  9.2 1.0 copy-start
  107.6 1.8 %copy-start.1 = (bf16[160,2048]{1,0:T(8,128)(2,1)S(1)}, bf16[160,2048]{1,0:T(8,128)(2,1)}, u32[]{:S(2)}) copy-start(bf16[160,2048]{1,0:T(8,128)(2,1)} %get-tuple-element.7) | copy-start | bytes 1966084

commit v6 on v5

--- a/solution.py
+++ b/solution.py
@@ -107,28 +107,34 @@
     even = lax.rem(me, 2) == 0
     odd = jnp.logical_not(even)
 
-    def slab_copy(source, sem, target, landing):
+    parts = 4
+    size = rows // parts
+
+    def part_of(p):
+        return pl.ds(pl.multiple_of(p * size, size), size)
+
+    def slab_copy(p, source, sem, target, landing):
         return pltpu.make_async_remote_copy(
-            src_ref=source,
-            dst_ref=slabs.at[offsets.index(landing)],
-            send_sem=slab_send.at[sem],
-            recv_sem=slab_recv.at[offsets.index(landing)],
+            src_ref=source.at[part_of(p)],
+            dst_ref=slabs.at[offsets.index(landing), part_of(p)],
+            send_sem=slab_send.at[sem * parts + p],
+            recv_sem=slab_recv.at[offsets.index(landing) * parts + p],
             device_id={"row": me + target},
             device_id_type=pl.DeviceIdType.MESH,
         )
 
     sends = [
-        (there(1), slab_copy(high_ref, 0, 1, -1)),
-        (there(-1), slab_copy(low_ref, 1, -1, 1)),
-        (jnp.logical_and(even, there(2)), slab_copy(high_ref, 2, 2, -2)),
-        (jnp.logical_and(odd, there(-2)), slab_copy(low_ref, 3, -2, 2)),
+        (there(1), (high_ref, 0, 1, -1)),
+        (there(-1), (low_ref, 1, -1, 1)),
+        (jnp.logical_and(even, there(2)), (high_ref, 2, 2, -2)),
+        (jnp.logical_and(odd, there(-2)), (low_ref, 3, -2, 2)),
     ]
     relays = [
         (
             jnp.logical_and(even, jnp.logical_and(there(-1), there(1))),
-            slab_copy(slabs.at[offsets.index(-1)], 4, 1, -2),
+            (slabs.at[offsets.index(-1)], 4, 1, -2),
         ),
-        (jnp.logical_and(odd, there(1)), slab_copy(slabs.at[offsets.index(1)], 5, -1, 2)),
+        (jnp.logical_and(odd, there(1)), (slabs.at[offsets.index(1)], 5, -1, 2)),
     ]
 
     def pack_copy(d, landing):
@@ -141,8 +147,9 @@
             device_id_type=pl.DeviceIdType.MESH,
         )
 
-    for needed, copy in sends:
-        pl.when(needed)(copy.start)
+    for p in range(parts):
+        for needed, route in sends:
+            pl.when(needed)(lambda p=p, route=route: slab_copy(p, *route).start())
 
     w_in = w_in_ref[...]
     w_in_t = w_in_t_ref[...]
@@ -176,19 +183,19 @@
 
     looped(0, edge, 2, project_own)
 
-    def project_slab(d, relay):
+    def project_slab(p, d, relay):
         index = offsets.index(d)
         count = (slots - abs(d)) * edge
         skipped = max(0, -d - 1) * edge
         first = max(0, d) * edge
 
         def absent():
-            slabs[index] = jnp.zeros((rows, lanes), BF16)
-
-        pl.when(there(d))(lambda: slab_copy(low_ref, 0, d, d).wait_recv())
+            slabs[index, part_of(p), :] = jnp.zeros((size, lanes), BF16)
+
+        pl.when(there(d))(lambda: slab_copy(p, low_ref, 0, d, d).wait_recv())
         pl.when(jnp.logical_not(there(d)))(absent)
         if relay is not None:
-            pl.when(relay[0])(relay[1].start)
+            pl.when(relay[0])(lambda: slab_copy(p, *relay[1]).start())
 
         def placed(values):
             parts = [values[:, skipped : skipped + count]]
@@ -213,10 +220,15 @@
 
             return store
 
-        looped(0, edge // 4, 1, project_far)
-
-    pl.when(even)(lambda: project_slab(1, None))
-    pl.when(odd)(lambda: project_slab(-1, None))
+        blocks = edge // 4 // parts
+        looped(p * blocks, (p + 1) * blocks, 1, project_far)
+
+    def same_chip(p, carry):
+        pl.when(even)(lambda: project_slab(p, 1, None))
+        pl.when(odd)(lambda: project_slab(p, -1, None))
+        return carry
+
+    lax.fori_loop(0, parts, same_chip, 0)
 
     def piece(block):
         return pl.ds(pl.multiple_of(block * 128, 128), 128)
@@ -233,10 +245,14 @@
 
     looped(0, rows // 128, 2, cot_to_rows)
     looped(0, channels, 4, cot_to_blocks)
-    pl.when(even)(lambda: project_slab(-1, relays[0]))
-    pl.when(odd)(lambda: project_slab(1, relays[1]))
-    project_slab(-2, None)
-    project_slab(2, None)
+    def other_chip(p, carry):
+        pl.when(even)(lambda: project_slab(p, -1, relays[0]))
+        pl.when(odd)(lambda: project_slab(p, 1, relays[1]))
+        project_slab(p, -2, None)
+        project_slab(p, 2, None)
+        return carry
+
+    lax.fori_loop(0, parts, other_chip, 0)
 
     def triangle(c):
         every = pl.ds(c, edge, stride=channels)
@@ -400,8 +416,9 @@
 
     summed(late, 4 * channels, steps, beside_late)
 
-    for needed, copy in sends + relays:
-        pl.when(needed)(copy.wait_send)
+    for p in range(parts):
+        for needed, route in sends + relays:
+            pl.when(needed)(lambda p=p, route=route: slab_copy(p, *route).wait_send())
     for d in offsets:
         pl.when(there(d))(lambda d=d: pack_copy(d, -d).wait_send())
 
@@ -456,8 +473,8 @@
             pltpu.VMEM((far, rows * edge // lanes, lanes), F32),
             pltpu.VMEM((steps, channels, 6 * channels), F32),
             pltpu.VMEM((steps, channels, 6 * channels), F32),
-            pltpu.SemaphoreType.DMA((far + 2,)),
-            pltpu.SemaphoreType.DMA((far,)),
+            pltpu.SemaphoreType.DMA((4 * (far + 2),)),
+            pltpu.SemaphoreType.DMA((4 * far,)),
             pltpu.SemaphoreType.DMA((far,)),
             pltpu.SemaphoreType.DMA((far,)),
             pltpu.SemaphoreType.DMA((2 * steps,)),

time: 111 us -> 108 us (0.973)
  Pallas kernels: 90 us -> 87.1 us
    pallas_call x1, Pallas kernels: 90 us -> 87.1 us  [local(): pl.pallas_call(functools.partial(body, devices, slots, edge, channels), o...]
where the time goes in v6:
time: 108 us; the launch traced here: 107 us
  Pallas kernels  87.1 us (81%)
  local copies, waits for them, and re-layouts  17.8 us (16%)
  other arithmetic  1.78 us (2%)
    pallas_call x1, Pallas kernels, local(): pl.pallas_call(functools.partial(body, devices, slots, edge, channels), o...  87.1 us
    unnamed x7, local copies, waits for them, and re-layouts  4.75 us
    split x2, local copies, waits for them, and re-layouts, local(): jnp.split(weights, [2 * channels, 3 * channels, 4 * channels], axis=1)  2.31 us
    another operation x1, local copies, waits for them, and re-layouts, local(): tiles = pair[0].reshape(slots, edge, edge, channels)  2.3 us

profile of v6, /device:TPU:0, one launch (start us, length us, event | category | flops | bytes accessed | tf_op | source)
XLA Modules:
  0.0 107.4 jit_solution(10665666764538941697)
XLA Ops:
  0.6 0.7 convert_bitcast_fusion
  1.4 0.1 broadcast_in_dim.4
  1.4 0.6 broadcast_in_dim_reshape.3.mask_ref
  2.1 1.4 %copy.24 = bf16[64,64]{0,1:T(8,128)(2,1)} copy(bf16[64,64]{1,0:T(8,128)(2,1)} %w_out_ref.1) | data formatting | bytes 16384 | tf_op args[3]
  3.5 1.5 %copy.23 = bf16[64,320]{0,1:T(8,128)(2,1)} copy(bf16[64,320]{1,0:T(8,128)(2,1)} %w_in_ref.1) | data formatting | bytes 81920 | tf_op args[2]
  5.0 2.3 %reshape_squeeze.6 = bf16[5,32,32,64]{3,2,1,0:T(8,128)(2,1)S(1)} reshape(bf16[1,5,32,2048]{3,2,1,0:T(8,128)(2,1)} %param.5) | data formatting | bytes 1310720 | tf_op jit(solution)/shard_map/reshape;squeeze | solution.py:443
  7.3 0.4 fusion
  7.7 1.0 reshape.27
  8.7 0.5 copy.25.own_ref
  9.2 0.0 copy-start
  9.2 1.0 copy-done
  10.2 1.2 %fusion.1 = (bf16[2048,128]{1,0:T(8,128)(2,1)}, bf16[2048,128]{1,0:T(8,128)(2,1)}) fusion(bf16[2048,160]{1,0:T(8,128)(2,1)S(1)} %copy.25.own_ref), kind=kLoop, calls=%fused_computation.5 | loop fusion | bytes 2097152 | tf_op jit(solution)/shard_map/slice | solution.py:447
  11.4 87.1 %shard_map.84 = (bf16[160,2048]{1,0:T(8,128)(2,1)}, bf16[2048,160]{1,0:T(8,128)(2,1)}, f32[64,384]{1,0:T(8,128)}) custom-call(bf16[2048,160]{1,0:T(8,128)(2,1)} %copy-done, bf16[2048,128]{1,0:T(8,128)(2,1)} %get-tuple-element.11.low_ref, bf16[2048,128]{1,0:T(8,128)(2,1)} %get-tuple-element.10.high_ref, bf16[160,2048]{1,0:T(8,128)(2,1)} %bitcast.23, ...), custom_call_target="tpu_custom_call" | custom-call | tf_op jit(solution)/shard_map/pallas_call | solution.py:451
  98.5 1.5 %fusion.2 = (f32[64,64]{1,0:T(8,128)}, f32[64,64]{1,0:T(8,128)S(1)}) fusion(f32[64,384]{1,0:T(8,128)} %get-tuple-element.9), kind=kLoop, calls=%fused_computation.6 | loop fusion | bytes 65536 | tf_op jit(solution)/shard_map/split | solution.py:487
  100.0 0.8 fusion.3
  100.8 0.6 pad_maximum_fusion
  101.4 1.4 %copy.26 = bf16[2048,160]{0,1:T(8,128)(2,1)S(1)} copy(bf16[2048,160]{1,0:T(8,128)(2,1)} %get-tuple-element.8) | data formatting | bytes 1310720 | tf_op jit(solution)/shard_map/pallas_call | solution.py:451
  102.9 1.3 %reshape.29 = bf16[32,64,5,32]{1,0,3,2:T(8,128)(2,1)S(1)} reshape(bf16[2048,160]{0,1:T(8,128)(2,1)S(1)} %copy.26) | data formatting | bytes 1310720 | tf_op jit(solution)/shard_map/reshape | solution.py:440
  104.2 0.5 copy.27
  104.7 0.0 copy-start.1
  104.7 1.8 %reshape.30 = bf16[1,5,32,2048]{3,2,1,0:T(8,128)(2,1)} reshape(bf16[5,32,32,64]{3,2,1,0:T(8,128)(2,1)S(1)} %copy.27) | data formatting | bytes 1310720 | tf_op jit(solution)/shard_map/reshape | solution.py:441
  106.5 0.0 copy-done.1
  106.5 0.8 copy.32
Async XLA Ops:
  9.2 1.0 copy-start
  104.7 1.8 %copy-start.1 = (bf16[160,2048]{1,0:T(8,128)(2,1)S(1)}, bf16[160,2048]{1,0:T(8,128)(2,1)}, u32[]{:S(2)}) copy-start(bf16[160,2048]{1,0:T(8,128)(2,1)} %get-tuple-element.7) | copy-start | bytes 1966084

commit v7 on v6

--- a/solution.py
+++ b/solution.py
@@ -383,36 +383,35 @@
 
     def to_pair(i):
         normed, scale = unit(own_ref[at(i), :].astype(F32))
-        result = unit_back(normed, scale, dot(w_in, d_projected[i], NN)).astype(BF16)
+        result = unit_back(normed, scale, dot(w_in, d_projected[i], NN))
+        return lambda: put(d_left, at(i), result)
+
+    def to_rows(source, target, c):
+        every = pl.ds(c, edge, stride=channels)
+        values = taken(source, every, wide)
+        values = jnp.concatenate([values[:, w * edge : (w + 1) * edge] for w in range(slots)], axis=0).T
+        return lambda: put(target, every, values)
+
+    def to_tiles(source, target, block):
+        values = taken(source, piece(block), wide).T.astype(BF16)
 
         def store():
-            grad_ref[at(i), :] = result
+            target[:, piece(block)] = values
 
         return store
 
-    def update_to_rows(c):
-        every = pl.ds(c, edge, stride=channels)
-        values = taken(gates, every, wide)
-        values = jnp.concatenate([values[:, w * edge : (w + 1) * edge] for w in range(slots)], axis=0).T
-        return lambda: put(tri, every, values)
-
-    def update_to_tiles(block):
-        values = taken(tri, piece(block), wide).T.astype(BF16)
-
-        def store():
-            update_ref[:, piece(block)] = values
-
-        return store
+    work = [
+        (edge, 2, to_pair),
+        (channels, 4, functools.partial(to_rows, d_left, d_right)),
+        (rows // 128, 2, functools.partial(to_tiles, d_right, grad_ref)),
+        (channels, 4, functools.partial(to_rows, gates, tri)),
+        (rows // 128, 2, functools.partial(to_tiles, tri, update_ref)),
+    ]
 
     def beside_late(step):
-        middle_step = steps // 2
-        if step < middle_step:
-            blocks = channels // 4
-            looped(blocks * step // middle_step * 4, blocks * (step + 1) // middle_step * 4, 4, update_to_rows)
-        else:
-            blocks, step_now, step_count = rows // 256, step - middle_step, steps - middle_step
-            looped(blocks * step_now // step_count * 2, blocks * (step_now + 1) // step_count * 2, 2, update_to_tiles)
-        looped(edge // 2 * step // steps * 2, edge // 2 * (step + 1) // steps * 2, 2, to_pair)
+        for place, (count, batch, compute) in enumerate(work):
+            if place * steps // len(work) == step:
+                looped(0, count, batch, compute)
 
     summed(late, 4 * channels, steps, beside_late)
 
@@ -436,10 +435,6 @@
     def to_columns(tiles):
         return jnp.transpose(tiles, (1, 3, 0, 2)).reshape(rows, wide)
 
-    def from_columns(columns):
-        tiles = columns.reshape(edge, channels, slots, edge)
-        return jnp.transpose(tiles, (2, 0, 3, 1)).reshape(pair.shape)
-
     tiles = pair[0].reshape(slots, edge, edge, channels)
     own = to_columns(tiles * kept[0].astype(BF16)[:, None, None, None])
     cot = cotangent[0].reshape(wide, rows)
@@ -452,7 +447,7 @@
         functools.partial(body, devices, slots, edge, channels),
         out_shape=(
             jax.ShapeDtypeStruct((wide, rows), BF16),
-            jax.ShapeDtypeStruct((rows, wide), BF16),
+            jax.ShapeDtypeStruct((wide, rows), BF16),
             jax.ShapeDtypeStruct((channels, 6 * channels), F32),
         ),
         in_specs=[whole] * 9,
@@ -489,7 +484,7 @@
     )
     grad_w_in = jnp.concatenate([first, second, gate], axis=1)
     grad_w_out = out
-    return (update.reshape(pair.shape), from_columns(grad), grad_w_in, grad_w_out)
+    return (update.reshape(pair.shape), grad.reshape(pair.shape), grad_w_in, grad_w_out)
 
 
 def solution(mesh):

time: 108 us -> 110 us (1.019)
  Pallas kernels: 87.1 us -> 92.4 us
  local copies, waits for them, and re-layouts: 17.8 us -> 14.8 us
    pallas_call x1, Pallas kernels: 87.1 us -> 92.4 us  [local(): pl.pallas_call(functools.partial(body, devices, slots, edge, channels), o...]
    reshape x2 -> x0, local copies, waits for them, and re-layouts: 3.15 us -> none  [the longest x1 1.82 us: from_columns(): return jnp.transpose(tiles, (2, 0, 3, 1)).reshape(pair.shape)]
    unnamed x7 -> x8, local copies, waits for them, and re-layouts: 4.75 us -> 6.73 us
    pallas_call x1 -> x0, local copies, waits for them, and re-layouts: 1.41 us -> none  [local(): pl.pallas_call(functools.partial(body, devices, slots, edge, channels), o...]
where the time goes in v7:
time: 110 us
  Pallas kernels  92.4 us (84%)
  local copies, waits for them, and re-layouts  14.8 us (13%)
  other arithmetic  1.78 us (2%)
    pallas_call x1, Pallas kernels, local(): pl.pallas_call(functools.partial(body, devices, slots, edge, channels), o...  92.4 us
    unnamed x8, local copies, waits for them, and re-layouts  6.73 us
    split x2, local copies, waits for them, and re-layouts, local(): jnp.split(weights, [2 * channels, 3 * channels, 4 * channels], axis=1)  2.31 us
    another operation x1, local copies, waits for them, and re-layouts, local(): tiles = pair[0].reshape(slots, edge, edge, channels)  2.3 us

profile of v7, /device:TPU:0, one launch (start us, length us, event | category | flops | bytes accessed | tf_op | source)
XLA Modules:
  0.0 109.6 jit_solution(13878347914832787745)
XLA Ops:
  0.6 0.7 convert_bitcast_fusion
  1.4 0.1 broadcast_in_dim.4
  1.4 0.7 broadcast_in_dim_reshape.3.mask_ref
  2.1 1.4 %copy.16 = bf16[64,64]{0,1:T(8,128)(2,1)} copy(bf16[64,64]{1,0:T(8,128)(2,1)} %w_out_ref.1) | data formatting | bytes 16384 | tf_op args[3]
  3.5 1.5 %copy.15 = bf16[64,320]{0,1:T(8,128)(2,1)} copy(bf16[64,320]{1,0:T(8,128)(2,1)} %w_in_ref.1) | data formatting | bytes 81920 | tf_op args[2]
  5.0 2.3 %reshape_squeeze.6 = bf16[5,32,32,64]{3,2,1,0:T(8,128)(2,1)S(1)} reshape(bf16[1,5,32,2048]{3,2,1,0:T(8,128)(2,1)} %param.5) | data formatting | bytes 1310720 | tf_op jit(solution)/shard_map/reshape;squeeze | solution.py:438
  7.3 0.4 fusion
  7.7 1.0 reshape.24
  8.7 0.5 copy.17.own_ref
  9.2 0.0 copy-start
  9.2 1.0 copy-done
  10.2 1.2 %fusion.1 = (bf16[2048,128]{1,0:T(8,128)(2,1)}, bf16[2048,128]{1,0:T(8,128)(2,1)}) fusion(bf16[2048,160]{1,0:T(8,128)(2,1)S(1)} %copy.17.own_ref), kind=kLoop, calls=%fused_computation.5 | loop fusion | bytes 2097152 | tf_op jit(solution)/shard_map/slice | solution.py:442
  11.4 92.4 %shard_map.84 = (bf16[160,2048]{1,0:T(8,128)(2,1)}, bf16[160,2048]{1,0:T(8,128)(2,1)}, f32[64,384]{1,0:T(8,128)}) custom-call(bf16[2048,160]{1,0:T(8,128)(2,1)} %copy-done, bf16[2048,128]{1,0:T(8,128)(2,1)} %get-tuple-element.11.low_ref, bf16[2048,128]{1,0:T(8,128)(2,1)} %get-tuple-element.10.high_ref, bf16[160,2048]{1,0:T(8,128)(2,1)} %bitcast.19, ...), custom_call_target="tpu_custom_call" | custom-call | tf_op jit(solution)/shard_map/pallas_call | solution.py:446
  103.8 0.0 copy-start.1
  103.9 1.5 %fusion.2 = (f32[64,64]{1,0:T(8,128)}, f32[64,64]{1,0:T(8,128)S(1)}) fusion(f32[64,384]{1,0:T(8,128)} %get-tuple-element.9), kind=kLoop, calls=%fused_computation.6 | loop fusion | bytes 65536 | tf_op jit(solution)/shard_map/split | solution.py:482
  105.4 0.8 fusion.3
  106.2 0.6 pad_maximum_fusion
  106.8 2.0 %copy.23 = bf16[1,5,32,2048]{3,2,1,0:T(8,128)(2,1)} copy(bf16[1,5,32,2048]{3,2,1,0:T(8,128)(2,1)} %bitcast.18) | data formatting | bytes 1310720
  108.8 0.0 copy-done.1
  108.8 0.8 copy.24
Async XLA Ops:
  9.2 1.0 copy-start
  103.8 5.0 %copy-start.1 = (bf16[160,2048]{1,0:T(8,128)(2,1)S(1)}, bf16[160,2048]{1,0:T(8,128)(2,1)}, u32[]{:S(2)}) copy-start(bf16[160,2048]{1,0:T(8,128)(2,1)} %get-tuple-element.8) | copy-start | bytes 1966084

commit v8 on v6

--- a/solution.py
+++ b/solution.py
@@ -244,7 +244,7 @@
         return lambda: put(d_right, every, values)
 
     looped(0, rows // 128, 2, cot_to_rows)
-    looped(0, channels, 4, cot_to_blocks)
+    looped(0, channels, 8, cot_to_blocks)
     def other_chip(p, carry):
         pl.when(even)(lambda: project_slab(p, -1, relays[0]))
         pl.when(odd)(lambda: project_slab(p, 1, relays[1]))
@@ -265,7 +265,7 @@
 
         return store
 
-    looped(0, channels, 4, triangle)
+    looped(0, channels, 8, triangle)
 
     def middle(start, carry):
         total = carry
@@ -301,7 +301,7 @@
         result = dot(taken(tri, every, wide).astype(BF16), band[c], NN)
         return lambda: put(d_left, every, result)
 
-    looped(0, channels, 4, to_left)
+    looped(0, channels, 8, to_left)
 
     def weigh(group, ref, joined_gate):
         def compute(block, carry):

time: 108 us -> 107 us (level)
  Pallas kernels: 87.1 us -> 86 us
where the time goes in v8:
time: 107 us; the launch traced here: 106 us
  Pallas kernels  86 us (80%)
  local copies, waits for them, and re-layouts  17.8 us (17%)
  other arithmetic  1.78 us (2%)
    pallas_call x1, Pallas kernels, local(): pl.pallas_call(functools.partial(body, devices, slots, edge, channels), o...  86 us
    unnamed x7, local copies, waits for them, and re-layouts  4.75 us
    split x2, local copies, waits for them, and re-layouts, local(): jnp.split(weights, [2 * channels, 3 * channels, 4 * channels], axis=1)  2.31 us
    another operation x1, local copies, waits for them, and re-layouts, local(): tiles = pair[0].reshape(slots, edge, edge, channels)  2.3 us

profile of v8, /device:TPU:0, one launch (start us, length us, event | category | flops | bytes accessed | tf_op | source)
XLA Modules:
  0.0 106.3 jit_solution(2827426225637469441)
XLA Ops:
  0.6 0.7 convert_bitcast_fusion
  1.4 0.1 broadcast_in_dim.4
  1.4 0.6 broadcast_in_dim_reshape.3.mask_ref
  2.1 1.4 %copy.24 = bf16[64,64]{0,1:T(8,128)(2,1)} copy(bf16[64,64]{1,0:T(8,128)(2,1)} %w_out_ref.1) | data formatting | bytes 16384 | tf_op args[3]
  3.5 1.5 %copy.23 = bf16[64,320]{0,1:T(8,128)(2,1)} copy(bf16[64,320]{1,0:T(8,128)(2,1)} %w_in_ref.1) | data formatting | bytes 81920 | tf_op args[2]
  5.0 2.3 %reshape_squeeze.6 = bf16[5,32,32,64]{3,2,1,0:T(8,128)(2,1)S(1)} reshape(bf16[1,5,32,2048]{3,2,1,0:T(8,128)(2,1)} %param.5) | data formatting | bytes 1310720 | tf_op jit(solution)/shard_map/reshape;squeeze | solution.py:443
  7.3 0.4 fusion
  7.7 1.0 reshape.27
  8.7 0.5 copy.25.own_ref
  9.2 0.0 copy-start
  9.2 1.0 copy-done
  10.2 1.2 %fusion.1 = (bf16[2048,128]{1,0:T(8,128)(2,1)}, bf16[2048,128]{1,0:T(8,128)(2,1)}) fusion(bf16[2048,160]{1,0:T(8,128)(2,1)S(1)} %copy.25.own_ref), kind=kLoop, calls=%fused_computation.5 | loop fusion | bytes 2097152 | tf_op jit(solution)/shard_map/slice | solution.py:447
  11.4 86.0 %shard_map.84 = (bf16[160,2048]{1,0:T(8,128)(2,1)}, bf16[2048,160]{1,0:T(8,128)(2,1)}, f32[64,384]{1,0:T(8,128)}) custom-call(bf16[2048,160]{1,0:T(8,128)(2,1)} %copy-done, bf16[2048,128]{1,0:T(8,128)(2,1)} %get-tuple-element.11.low_ref, bf16[2048,128]{1,0:T(8,128)(2,1)} %get-tuple-element.10.high_ref, bf16[160,2048]{1,0:T(8,128)(2,1)} %bitcast.23, ...), custom_call_target="tpu_custom_call" | custom-call | tf_op jit(solution)/shard_map/pallas_call | solution.py:451
  97.4 1.5 %fusion.2 = (f32[64,64]{1,0:T(8,128)}, f32[64,64]{1,0:T(8,128)S(1)}) fusion(f32[64,384]{1,0:T(8,128)} %get-tuple-element.9), kind=kLoop, calls=%fused_computation.6 | loop fusion | bytes 65536 | tf_op jit(solution)/shard_map/split | solution.py:487
  98.9 0.8 fusion.3
  99.7 0.6 pad_maximum_fusion
  100.4 1.4 %copy.26 = bf16[2048,160]{0,1:T(8,128)(2,1)S(1)} copy(bf16[2048,160]{1,0:T(8,128)(2,1)} %get-tuple-element.8) | data formatting | bytes 1310720 | tf_op jit(solution)/shard_map/pallas_call | solution.py:451
  101.8 1.3 %reshape.29 = bf16[32,64,5,32]{1,0,3,2:T(8,128)(2,1)S(1)} reshape(bf16[2048,160]{0,1:T(8,128)(2,1)S(1)} %copy.26) | data formatting | bytes 1310720 | tf_op jit(solution)/shard_map/reshape | solution.py:440
  103.1 0.5 copy.27
  103.6 0.0 copy-start.1
  103.7 1.8 %reshape.30 = bf16[1,5,32,2048]{3,2,1,0:T(8,128)(2,1)} reshape(bf16[5,32,32,64]{3,2,1,0:T(8,128)(2,1)S(1)} %copy.27) | data formatting | bytes 1310720 | tf_op jit(solution)/shard_map/reshape | solution.py:441
  105.5 0.0 copy-done.1
  105.5 0.8 copy.32
Async XLA Ops:
  9.2 1.0 copy-start
  103.6 1.8 %copy-start.1 = (bf16[160,2048]{1,0:T(8,128)(2,1)S(1)}, bf16[160,2048]{1,0:T(8,128)(2,1)}, u32[]{:S(2)}) copy-start(bf16[160,2048]{1,0:T(8,128)(2,1)} %get-tuple-element.7) | copy-start | bytes 1966084
